TPU v7x, 256 devices: a whole 4x4x8 slice. The times are simulated.
256 devices in a mesh: ctx: 32 (over z, x), head: 8 (over y, core).
Axes of the slice: x: 4, y: 4, z: 8, core: 2. Of those that a mesh axis runs over, the one named last changes fastest.
Arguments:
- q_nope: bfloat16 [4096, 8192], P('ctx', 'head'), may hold values from -6 to 6
- q_rope: bfloat16 [4096, 4096], P('ctx', 'head'), may hold values from -300 to 300
- latent: bfloat16 [4096, 512], P('ctx'), may hold values from -6 to 6
- k_rope: bfloat16 [4096, 64], P('ctx'), may hold values from -4 to 4
- span_order: int32 [64], replicated, may hold values from 0 to 63, each once
- w_uk: bfloat16 [512, 8192], P(None, 'head'), may hold values from -0.25 to 0.25
- w_uv: bfloat16 [512, 8192], P(None, 'head'), may hold values from -0.25 to 0.25
- w_o: bfloat16 [8192, 7168], P('head', 'ctx'), may hold values from -0.125 to 0.125
Outputs:
- attended: bfloat16 [4096, 7168], P('ctx', 'head')
Inputs may be any that keep to these rules, and one draw needn't show every extreme that they name: `span_order`: a permutation of 0 to 63.
All inputs are finite; a program needn't handle non-finite values.
Results may differ from a plain program's by a relative error of at most 0.014.
Values may be sent and summed in bfloat16 or wider, within the bound.
A program may use at most 128 MiB of HBM per device.

v0:
```python
import math

import jax
import jax.numpy as jnp
from jax import lax
from jax.sharding import Mesh
from jax.sharding import PartitionSpec as P

LAT = 512
ROPE = 64
NOPE = 128
VDIM = 128
CTX = ("ctx_0", "ctx_1")


def gathered_by_axis(array, axes, dim):
    for axis in reversed(axes):
        array = lax.all_gather(array, axis, axis=dim, tiled=True)
    return array


def cut_along(array, dim, count):
    before, after = (array.shape[:dim], array.shape[dim + 1 :])
    return jnp.moveaxis(array.reshape(*before, count, -1, *after), dim, 0)


def sent_and_summed(array, axis, dim):
    parts = cut_along(array, dim, lax.axis_size(axis))
    arrived = lax.all_to_all(parts, axis, split_axis=0, concat_axis=0, tiled=True)
    return arrived.astype(jnp.float32).sum(axis=0)


def span_place(slot_ids, table):
    match = slot_ids[:, None] == jnp.arange(table.shape[0], dtype=jnp.int32)[None, :]
    return jnp.sum(jnp.where(match, table[None, :], 0), axis=1)


def local(q_nope, q_rope, latent, k_rope, span_order, w_uk, w_uv, w_o):
    rows = q_nope.shape[0]
    half = rows // 2
    heads = w_uk.shape[1] // NOPE
    scale = 1.0 / math.sqrt(NOPE + ROPE)
    local_rows = jnp.arange(rows, dtype=jnp.int32)
    query_slot = lax.axis_index(CTX) * 2 + local_rows // half
    qpos = span_place(query_slot, span_order) * half + local_rows % half
    absorbed = jnp.einsum(
        "thn,lhn->htl",
        q_nope.reshape(rows, heads, NOPE),
        w_uk.reshape(LAT, heads, NOPE),
        preferred_element_type=jnp.float32,
    ).astype(jnp.bfloat16)
    rotary = q_rope.reshape(rows, heads, ROPE)
    lat_piece = gathered_by_axis(latent, CTX, 0)
    rope_piece = gathered_by_axis(k_rope, CTX, 0)
    count = lat_piece.shape[0]
    key_rows = jnp.arange(count, dtype=jnp.int32)
    kpos = span_place(key_rows // half, span_order) * half + key_rows % half
    running = jnp.full((heads, rows), -1e30, jnp.float32)
    score = jnp.einsum("htl,kl->htk", absorbed, lat_piece, preferred_element_type=jnp.float32)
    score = score + jnp.einsum(
        "thr,kr->htk", rotary, rope_piece, preferred_element_type=jnp.float32
    )
    score = score * scale
    visible = kpos[None, None, :] <= qpos[None, :, None]
    newest = jnp.maximum(running, jnp.max(jnp.where(visible, score, -1e30), axis=-1))
    weight = jnp.where(visible, jnp.exp(score - newest[..., None]), 0.0)
    summed = jnp.sum(weight, axis=-1)
    accum = jnp.einsum(
        "htk,kl->htl", weight.astype(jnp.bfloat16), lat_piece, preferred_element_type=jnp.float32
    )
    running, summed, accum = (newest, summed, accum)
    context = (accum / summed[..., None]).astype(jnp.bfloat16)
    heads_out = jnp.einsum(
        "htl,lhv->thv", context, w_uv.reshape(LAT, heads, VDIM), preferred_element_type=jnp.float32
    ).astype(jnp.bfloat16)
    heads_out = heads_out.reshape(rows, heads * VDIM)
    partial_value = jnp.dot(
        heads_out, lax.all_gather(w_o, CTX, axis=1, tiled=True), preferred_element_type=jnp.float32
    ).astype(jnp.bfloat16)
    return sent_and_summed(partial_value, "head", 1).astype(jnp.bfloat16)


def solution(mesh):
    torus = Mesh(mesh.devices.reshape(8, 4, mesh.shape["head"]), ("ctx_0", "ctx_1", "head"))
    in_specs = (
        P(CTX, "head"),
        P(CTX, "head"),
        P(CTX, None),
        P(CTX, None),
        P(),
        P(None, "head"),
        P(None, "head"),
        P("head", CTX),
    )
    out_specs = P(CTX, "head")
    return jax.shard_map(local, mesh=torus, in_specs=in_specs, out_specs=out_specs, check_vma=False)
```

profile of v0, /device:TPU:16, one launch (start us, length us, event | category | flops | bytes accessed | tf_op | source)
XLA Modules:
  0.0 258.3 jit_solution(16271409168613144951)
XLA Ops:
  6.5 0.0 copy-start
  6.5 0.0 all-gather.3.cloned.1.call-start
  6.5 14.9 %all_gather.15 = bf16[512,512]{1,0:T(8,128)(2,1)} all-gather(bf16[128,512]{1,0:T(8,128)(2,1)} %param.10), channel_id=1, replica_groups=mesh['ctx_0'=8,'ctx_1'=4,'head'=8] {'ctx_1'}, dimensions={0}, use_global_device_ids=true | all-gather | bytes 655360 | tf_op jit(solution)/shard_map/all_gather | solution.py:18
  21.5 0.0 all-gather.3.cloned.1.call-update
  21.5 0.0 all-gather.5.cloned.1.call-start
  21.6 0.7 all-gather.5.cloned.1.call-update
  22.3 1.0 copy.23
  23.3 1.5 copy.28
  24.8 10.8 %all_gather.17 = bf16[512,64]{0,1:T(8,128)(2,1)S(1)} all-gather(bf16[128,64]{0,1:T(8,128)(2,1)} %param.11), channel_id=1, replica_groups=mesh['ctx_0'=8,'ctx_1'=4,'head'=8] {'ctx_1'}, dimensions={0}, use_global_device_ids=true | all-gather | bytes 81920 | tf_op jit(solution)/shard_map/all_gather | solution.py:18
  35.6 0.7 select_reduce_fusion.2
  36.4 0.9 select_reduce_fusion.1
  37.3 30.6 %all_gather.18 = bf16[4096,64]{0,1:T(8,128)(2,1)S(1)} all-gather(bf16[512,64]{0,1:T(8,128)(2,1)S(1)} %all_gather.17), channel_id=1, replica_groups=mesh['ctx_0'=8,'ctx_1'=4,'head'=8] {'ctx_0'}, dimensions={0}, use_global_device_ids=true | all-gather | bytes 589824 | tf_op jit(solution)/shard_map/all_gather | solution.py:18
  67.9 0.4 broadcast_compare_fusion
  68.3 14.6 %all-gather.3.cloned.1.call-done = bf16[4096,512]{1,0:T(8,128)(2,1)} async-done(((bf16[512,512]{1,0:T(8,128)(2,1)}), bf16[4096,512]{1,0:T(8,128)(2,1)}) %all-gather.3.cloned.1.call-update) | async-done | bytes 4194320 | tf_op jit(solution)/shard_map/all_gather | solution.py:18
  82.8 0.0 copy-done
  82.8 10.2 %fusion.9 = f32[8,128,4096]{2,1,0:T(8,128)} fusion(bf16[4096,512]{1,0:T(8,128)(2,1)} %all-gather.3.cloned.1.call-done, bf16[512,1024]{1,0:T(8,128)(2,1)S(1)} %copy-done, bf16[128,1024]{1,0:T(8,128)(2,1)} %param.8), kind=kOutput, calls=%fused_computation.12 | convolution fusion | flops 4429709312 | bytes 22282240 | tf_op jit(solution)/shard_map/htl,kl->htk/dot_general | solution.py:59
  93.0 11.4 %select_reduce_fusion = (f32[8,128]{1,0:T(8,128)S(1)}, f32[8,128,4096]{2,1,0:T(8,128)}) fusion(pred[128,4096]{1,0:T(8,128)(4,1)S(1)} %broadcast_compare_fusion, f32[8,128,4096]{2,1,0:T(8,128)} %fusion.9, bf16[128,8,64]{0,2,1:T(8,128)(2,1)S(1)} %bitcast.57, bf16[4096,64]{0,1:T(8,128)(2,1)S(1)} %all_gather.18), kind=kOutput, calls=%fused_computation.3 | convolution fusion | flops 553647104 | bytes 34738176 | tf_op jit(solution)/shard_map/thr,kr->htk/dot_general | solution.py:60
  104.5 9.3 %fusion.1 = f32[8,128]{1,0:T(8,128)S(1)} fusion(f32[8,128,4096]{2,1,0:T(8,128)} %get-tuple-element.6, f32[8,128]{1,0:T(8,128)S(1)} %broadcast_maximum_fusion, pred[128,4096]{1,0:T(8,128)(4,1)S(1)} %broadcast_compare_fusion), kind=kLoop, calls=%fused_computation.4 | loop fusion | flops 12581888 | bytes 17309696 | tf_op jit(solution)/shard_map/reduce_sum | solution.py:67
  113.7 11.9 %fusion.20 = bf16[8,128,128]{1,2,0:T(8,128)(2,1)S(1)} fusion(bf16[512,8,128]{0,2,1:T(8,128)(2,1)S(1)} %bitcast.56, bf16[4096,512]{1,0:T(8,128)(2,1)} %all-gather.3.cloned.1.call-done, f32[8,128,4096]{2,1,0:T(8,128)} %get-tuple-element.6, f32[8,128]{1,0:T(8,128)S(1)} %broadcast_maximum_fusion, pred[128,4096]{1,0:T(8,128)(4,1)S(1)} %broadcast_compare_fusion, ...), kind=kOutput, calls=%fused_computation.18 | convolution fusion | flops 4442947584 | bytes 22814720 | tf_op jit(solution)/shard_map/htl,lhv->thv/dot_general | solution.py:73
  125.6 88.4 %all-gather.5.cloned.1.call-done = bf16[1024,7168]{0,1:T(8,128)(2,1)} async-done(((bf16[1024,224]{0,1:T(8,128)(2,1)}), bf16[1024,7168]{0,1:T(8,128)(2,1)}) %all-gather.5.cloned.1.call-update) | async-done | bytes 14680080 | tf_op jit(solution)/shard_map/all_gather | solution.py:78
  214.0 10.1 %convolution_convert_fusion = bf16[128,7168]{1,0:T(8,128)(2,1)S(1)} fusion(bf16[128,1024]{0,1:T(8,128)(2,1)S(1)} %bitcast.58, bf16[1024,7168]{0,1:T(8,128)(2,1)} %all-gather.5.cloned.1.call-done), kind=kOutput, calls=%fused_computation.6 | convolution fusion | flops 1879965696 | bytes 16777216 | tf_op jit(solution)/shard_map/dot_general | solution.py:77
  224.2 0.2 copy.43
  224.4 26.1 %all_to_all.5 = bf16[8,128,896]{2,1,0:T(8,128)(2,1)S(1)} all-to-all(bf16[8,128,896]{2,1,0:T(8,128)(2,1)S(1)} %bitcast.54), channel_id=1, replica_groups=mesh['ctx_0'=8,'ctx_1'=4,'head'=8] {'head'}, dimensions={0} | all-to-all | bytes 3670016 | tf_op jit(solution)/shard_map/all_to_all | solution.py:29
  250.5 1.0 reduce_sum.42
  (5 shorter events, 0.0 us)
Async XLA Ops:
  6.5 76.3 %copy-start = (bf16[512,1024]{1,0:T(8,128)(2,1)S(1)}, bf16[512,1024]{1,0:T(8,128)(2,1)}, u32[]{:S(2)}) copy-start(bf16[512,1024]{1,0:T(8,128)(2,1)} %param.13) | copy-start | bytes 3145732
  6.5 76.3 %all-gather.3.cloned.1.call-start = ((), (), s32[]{:S(2)}) async-start(), calls=%async_computation.1 | async-start | bytes 4718592 | tf_op jit(solution)/shard_map/all_gather | solution.py:18
  21.5 192.5 %all-gather.5.cloned.1.call-start = ((), (), s32[]{:S(2)}) async-start(), calls=%async_computation.2 | async-start | bytes 15138816 | tf_op jit(solution)/shard_map/all_gather | solution.py:78
Sparse Core Ops, SparseCore 0:
  21.6 61.1 all-gather.2
  85.4 128.5 all-gather.4
where the time goes:
time: 262 us; the launch traced here: 258 us
  waiting for transfers between devices  104 us (40%)
  blocking collectives  82.5 us (31%)
  matrix products  43.6 us (17%)
  between operations  13.5 us (5%)
  other arithmetic  12.3 us (5%)
  local copies, waits for them, and re-layouts  2.77 us (1%)
    all_gather x1, waiting for transfers between devices, local(): lax.all_gather(w_o, CTX, axis=1, tiled=True)  88.4 us
    all_gather x3, blocking collectives, gathered_by_axis(): array = lax.all_gather(array, axis, axis=dim, tiled=True)  56.4 us
    all_to_all x1, blocking collectives, sent_and_summed(): lax.all_to_all(parts, axis, split_axis=0, concat_axis=0, tiled=True)  26.1 us
    all_gather x1, waiting for transfers between devices, gathered_by_axis(): array = lax.all_gather(array, axis, axis=dim, tiled=True)  14.6 us
    dot_general x1, matrix products, local(): jnp.einsum('htl,lhv->thv', context, w_uv.reshape(LAT, heads, VDIM), prefe...  11.9 us
    dot_general x1, matrix products, local(): jnp.einsum('thr,kr->htk', rotary, rope_piece, preferred_element_type=jnp....  11.4 us
    dot_general x1, matrix products, local(): jnp.einsum('htl,kl->htk', absorbed, lat_piece, preferred_element_type=jnp...  10.2 us
    dot_general x1, matrix products, local(): jnp.dot(heads_out, lax.all_gather(w_o, CTX, axis=1, tiled=True), preferre...  10.1 us
  transfers between devices with their start and end apart: 2, of which 2 were waited for; matrix products, arithmetic and copies ran while one was open for 18% of the time, Pallas kernels for 0%

commit v1 on v0

v1 whole, which is shorter than its diff:
```python
import functools
import math

import jax
import jax.numpy as jnp
from jax import lax
from jax.experimental import pallas as pl
from jax.experimental.pallas import tpu as pltpu
from jax.sharding import Mesh
from jax.sharding import PartitionSpec as P

NZ, NX, NY = 8, 4, 4
TOK, SPAN = 128, 64
HEADS, NOPE, ROPE, LAT, VDIM = 8, 128, 64, 512, 128
WIDE = LAT + 2 * ROPE
COLS = 224
PAIRS = HEADS // 2
KEYS = NZ * NX * TOK
CHUNK = 512
FACTOR = math.log2(math.e) / math.sqrt(NOPE + ROPE)
HIDDEN = -1e30
MESH = pl.DeviceIdType.MESH
DELTAS = (0, -1, 1, -2, 2, -3, 3, -4)


def nt_dot(a, b):
    return lax.dot_general(a, b, (((1,), (1,)), ((), ())), preferred_element_type=jnp.float32)


def nn_dot(a, b):
    return jnp.dot(a, b, preferred_element_type=jnp.float32)


def kernel(
    qn, qr, lat, kr, order, wuk, wuv, wo, out,
    kbuf, stage, own_rope, qaug, acc, wbuf, hog, c1s, c1r, c2s, c2r, c3s, c3r,
    shift_sem, z_sem, w_sem, p_sem, o_sem, a_sem, c1_sem, c2_sem, c3_sem,
):
    z, x, y, core = (lax.axis_index(n) for n in ("z", "x", "y", "core"))
    other = 1 - core

    def at(dz=0, dx=0, dy=0):
        return (lax.rem(z + NZ + dz, NZ), lax.rem(x + NX + dx, NX), lax.rem(y + NY + dy, NY), core)

    partner = (z, x, y, other)
    peers = [at(dz=1), at(dz=-1), partner]
    peers += [at(dx=d) for d in (1, 2, 3)] + [at(dy=d) for d in (1, 2, 3)]
    barrier = pltpu.get_barrier_semaphore()
    for peer in peers:
        pl.semaphore_signal(barrier, inc=1, device_id=peer, device_id_type=MESH)

    sent = []

    def copy(src, dst, sems, device):
        return pltpu.make_async_remote_copy(
            src_ref=src, dst_ref=dst, send_sem=sems[0], recv_sem=sems[1], device_id=device, device_id_type=MESH
        )

    def send(src, dst, sems, device):
        made = copy(src, dst, sems, device)
        made.start()
        sent.append(made)

    def arrived(dst, sems, device):
        copy(dst, dst, sems, device).wait_recv()

    def pair_of(sems, *index):
        return sems.at[(0, *index)], sems.at[(1, *index)]

    own_slot = (z * NX + x) * 2 + core
    lane = lax.broadcasted_iota(jnp.int32, (SPAN, 2 * ROPE), 1)
    own_rope[...] = jnp.zeros_like(own_rope)
    own_rope[:, :ROPE] = kr[...]
    mine = pl.ds(pl.multiple_of(core * SPAN, SPAN), SPAN)
    stage[:, :LAT] = lat[mine, :]
    stage[:, LAT:] = jnp.where(
        lane == ROPE + own_slot, 1.0, own_rope[mine, :].astype(jnp.float32)
    ).astype(jnp.bfloat16)

    pl.semaphore_wait(barrier, len(peers))

    def sigma(k):
        return 1 - 2 * k

    def piece(k, delta, off):
        zz = lax.rem(z + NZ + sigma(k) * delta, NZ)
        xx = lax.rem(x + y * k + off + NX, NX)
        start = ((zz * NX + xx) * 2 + k) * SPAN
        return kbuf.at[pl.ds(pl.multiple_of(start, SPAN), SPAN)]

    def wdev(step):
        return at(dx=other * step, dy=core * step)

    zdev = {True: at(dz=sigma(core)), False: at(dz=-sigma(core))}
    own_rows = pl.ds(pl.multiple_of(own_slot * SPAN, SPAN), SPAN)
    shift_dev = at(dx=-(core * y))
    shift = copy(stage, kbuf.at[own_rows], (shift_sem.at[0], shift_sem.at[1]), shift_dev)

    @pl.when(core * y == 0)
    def _():
        kbuf[own_rows, :] = stage[...]

    @pl.when(core * y != 0)
    def _():
        shift.start()
        arrived(piece(core, 0, 0), (shift_sem.at[0], shift_sem.at[1]), shift_dev)

    def spread(i, delta):
        here = piece(core, delta, 0)
        for step, side in ((1, 0), (-1, 1)):
            send(here, here, pair_of(w_sem, side, i), wdev(step))
        send(here, here, pair_of(p_sem, 0, i), partner)

    for i, delta in enumerate(DELTAS):
        here = piece(core, delta, 0)
        if i:
            arrived(here, pair_of(z_sem, i), zdev[delta > 0])
        for later in range(i + 1, NZ):
            if (i == 0 and later < 3) or (i > 0 and later == i + 2):
                send(here, here, pair_of(z_sem, later), zdev[DELTAS[later] < 0])
        spread(i, delta)

    def wpart(delta, half):
        zz = lax.rem(z + NZ + sigma(core) * delta, NZ)
        return wbuf.at[zz, pl.ds(half * 512, 512)]

    for half in range(2):
        for later in (1, 2):
            send(wo.at[pl.ds(half * 512, 512)], wpart(0, half), pair_of(o_sem, half, later), zdev[DELTAS[later] < 0])
    wbuf[z] = wo[...]

    def serve_w(i):
        for half in range(2):
            here = wpart(DELTAS[i], half)
            arrived(here, pair_of(o_sem, half, i), zdev[DELTAS[i] > 0])
            if i + 2 < NZ:
                send(here, here, pair_of(o_sem, half, i + 2), zdev[DELTAS[i + 2] < 0])

    wide_lane = lax.broadcasted_iota(jnp.int32, (1, 2 * ROPE), 1)
    places = jnp.concatenate([order[...], order[...]], axis=1)
    half_of = lax.broadcasted_iota(jnp.int32, (TOK, 2 * ROPE), 0) // SPAN
    hidden = []
    for half in range(2):
        slot = (z * NX + x) * 2 + half
        place = jnp.sum(jnp.where(wide_lane == slot, places, 0), axis=1, keepdims=True)
        hidden.append(jnp.where(places >= place, HIDDEN, 0.0))
    mask = jnp.where(half_of == 0, hidden[0], hidden[1])
    low = lax.broadcasted_iota(jnp.int32, (TOK, 2 * ROPE), 1) < ROPE
    for h in range(HEADS):
        rows = pl.ds((h % 2) * TOK, TOK)
        cols = pl.ds(h * NOPE, NOPE)
        qaug[h // 2, rows, :LAT] = nt_dot(qn[:, cols], wuk[:, cols]).astype(jnp.bfloat16)
        rot = qr[:, pl.ds((h // 2) * 2 * ROPE, 2 * ROPE)].astype(jnp.float32)
        if h % 2:
            rot = pltpu.roll(rot, ROPE, 1)
        qaug[h // 2, rows, LAT:] = jnp.where(low, rot, mask).astype(jnp.bfloat16)

    for i, delta in enumerate(DELTAS):
        left, right = piece(core, delta, -1), piece(core, delta, 1)
        arrived(left, pair_of(w_sem, 0, i), wdev(-1))
        arrived(right, pair_of(w_sem, 1, i), wdev(1))
        parity = lax.rem(z + NZ + delta, 2)
        onward = piece(core, delta, 2 * parity - 1)
        send(onward, onward, pair_of(w_sem, 2, i), wdev(1 - 2 * parity))
        send(left, left, pair_of(p_sem, 1, i), partner)
        send(right, right, pair_of(p_sem, 2, i), partner)
    for i, delta in enumerate(DELTAS):
        far = piece(core, delta, 2)
        arrived(far, pair_of(w_sem, 2, i), wdev(1))
        send(far, far, pair_of(p_sem, 3, i), partner)
    for n, off in enumerate((0, -1, 1, 2)):
        for i, delta in enumerate(DELTAS):
            arrived(piece(other, delta, off), pair_of(p_sem, n, i), partner)

    row = lax.rem(lax.broadcasted_iota(jnp.int32, (2 * TOK, TOK), 0), TOK)
    col = lax.broadcasted_iota(jnp.int32, (2 * TOK, TOK), 1)
    seen = (col <= row) & (col >= (row // SPAN) * SPAN)

    for g in range(PAIRS):
        first = nt_dot(qaug[g, :, :LAT], lat[...]) + nt_dot(qaug[g, :, LAT:], own_rope[...])
        first = jnp.where(seen, first * FACTOR, HIDDEN)
        top = jnp.max(first, axis=1, keepdims=True)
        weight = jnp.exp2(first - top)
        total = jnp.sum(weight, axis=1, keepdims=True)
        acc[...] = nn_dot(weight.astype(jnp.bfloat16), lat[...])

        def body(n, carry):
            top, total = carry
            spots = [pl.ds(pl.multiple_of((2 * n + k) * CHUNK, CHUNK), CHUNK) for k in range(2)]
            scores = [nt_dot(qaug[g], kbuf[spot, :]) * FACTOR for spot in spots]
            for spot, score in zip(spots, scores):
                newest = jnp.maximum(top, jnp.max(score, axis=1, keepdims=True))
                shrink = jnp.exp2(top - newest)
                weight = jnp.exp2(score - newest)
                total = total * shrink + jnp.sum(weight, axis=1, keepdims=True)
                acc[...] = acc[...] * shrink + nn_dot(weight.astype(jnp.bfloat16), kbuf[spot, :LAT])
                top = newest
            return top, total

        top, total = lax.fori_loop(0, KEYS // (2 * CHUNK), body, (top, total))
        context = (acc[...] / total).astype(jnp.bfloat16)
        for k in range(2):
            cols = pl.ds((2 * g + k) * VDIM, VDIM)
            done = nn_dot(context[k * TOK : (k + 1) * TOK], wuv[:, cols])
            hog[g, x, :, k * VDIM : (k + 1) * VDIM] = done.astype(jnp.bfloat16)
        for d in (2, 1, 3):
            send(hog.at[g, x], hog.at[g, x], pair_of(a_sem, g, d), at(dx=d))
        if g == 0:
            serve_w(1)
            serve_w(2)
        if g == PAIRS - 1:
            serve_w(3)
            serve_w(4)

    for g in range(PAIRS):
        for d in (1, 2, 3):
            arrived(hog.at[g, lax.rem(x + NX - d, NX)], pair_of(a_sem, g, d), at(dx=-d))

    def project(zz):
        total = None
        for g in range(PAIRS):
            term = nn_dot(hog[g].reshape(NX * TOK, 2 * VDIM), wbuf[zz, pl.ds(g * 2 * VDIM, 2 * VDIM), :])
            total = term if total is None else total + term
        return total

    tilt = 1 - 2 * lax.rem(z, 2)
    ahead = []
    for n in range(NY):
        if n == 2:
            serve_w(5)
            serve_w(6)
        if n == 3:
            serve_w(7)
        step = (0, -tilt, tilt, 2)[n]
        j = lax.rem(z // 2 + NY + step, NY)
        c1s[n] = project(2 * j + other).astype(jnp.bfloat16)
        send(c1s.at[n], c1r.at[n], pair_of(c1_sem, n), partner)
        kept = project(2 * j + core)
        arrived(c1r.at[n], pair_of(c1_sem, n), partner)
        c2s[n] = (kept + c1r[n].astype(jnp.float32)).astype(jnp.bfloat16)
        onward = copy(c2s.at[n], c2r.at[y], (c2_sem.at[0, n], c2_sem.at[1, y]), (z, x, j, core))
        ahead.append((j, onward))

        @pl.when(j != y)
        def _():
            onward.start()

        @pl.when(j == y)
        def _():
            c2r[y] = c2s[n]

    for d in (1, 2, 3):
        yy = lax.rem(y + d, NY)
        arrived(c2r.at[yy], (c2_sem.at[0, 0], c2_sem.at[1, yy]), at(dy=d))
    summed = c2r[0].astype(jnp.float32)
    for k in range(1, NY):
        summed = summed + c2r[k].astype(jnp.float32)
    c3s[...] = summed.astype(jnp.bfloat16).reshape(NX, TOK, COLS)
    for d in (2, 1, 3):
        send(c3s.at[lax.rem(x + d, NX)], c3r.at[x], pair_of(c3_sem, d), at(dx=d))
    c3r[x] = c3s[x]
    for d in (1, 2, 3):
        arrived(c3r.at[lax.rem(x + NX - d, NX)], pair_of(c3_sem, d), at(dx=-d))
    out[...] = jnp.concatenate([c3r[k].astype(jnp.float32) for k in range(NX)], axis=1).astype(jnp.bfloat16)

    @pl.when(core * y != 0)
    def _():
        shift.wait_send()

    for j, onward in ahead:

        @pl.when(j != y)
        def _():
            onward.wait_send()

    for made in sent:
        made.wait_send()


def local(q_nope, q_rope, latent, k_rope, span_order, w_uk, w_uv, w_o):
    bf16, f32 = jnp.bfloat16, jnp.float32
    dma = pltpu.SemaphoreType.DMA
    vmem = pl.BlockSpec(memory_space=pltpu.VMEM)
    return pl.pallas_call(
        kernel,
        out_shape=jax.ShapeDtypeStruct((TOK, NX * COLS), bf16),
        in_specs=[vmem] * 8,
        out_specs=vmem,
        scratch_shapes=[
            pltpu.VMEM((KEYS, WIDE), bf16),
            pltpu.VMEM((SPAN, WIDE), bf16),
            pltpu.VMEM((TOK, 2 * ROPE), bf16),
            pltpu.VMEM((PAIRS, 2 * TOK, WIDE), bf16),
            pltpu.VMEM((2 * TOK, LAT), f32),
            pltpu.VMEM((NZ, HEADS * VDIM, COLS), bf16),
            pltpu.VMEM((PAIRS, NX, TOK, 2 * VDIM), bf16),
            pltpu.VMEM((NY, NX * TOK, COLS), bf16),
            pltpu.VMEM((NY, NX * TOK, COLS), bf16),
            pltpu.VMEM((NY, NX * TOK, COLS), bf16),
            pltpu.VMEM((NY, NX * TOK, COLS), bf16),
            pltpu.VMEM((NX, TOK, COLS), bf16),
            pltpu.VMEM((NX, TOK, COLS), bf16),
            dma((2,)),
            dma((2, NZ)),
            dma((2, 3, NZ)),
            dma((2, 4, NZ)),
            dma((2, 2, NZ)),
            dma((2, PAIRS, NX)),
            dma((2, NY)),
            dma((2, NY)),
            dma((2, NX)),
        ],
        compiler_params=pltpu.CompilerParams(
            collective_id=0, has_side_effects=True, vmem_limit_bytes=48 * 1024 * 1024
        ),
        cost_estimate=pl.CostEstimate(flops=11_000_000_000, bytes_accessed=4_000_000, transcendentals=4_200_000),
    )(q_nope, q_rope, latent, k_rope, span_order.reshape(1, -1), w_uk, w_uv, w_o)


def solution(mesh):
    torus = Mesh(mesh.devices.reshape(NZ, NX, NY, 2), ("z", "x", "y", "core"))
    ctx, head = ("z", "x"), ("y", "core")
    in_specs = (
        P(ctx, head),
        P(ctx, head),
        P(ctx, None),
        P(ctx, None),
        P(),
        P(None, head),
        P(None, head),
        P(head, ctx),
    )
    return jax.shard_map(local, mesh=torus, in_specs=in_specs, out_specs=P(ctx, head), check_vma=False)
```

time: 262 us -> 96.7 us (0.37); the launches traced: 258 us -> 96.4 us
  waiting for transfers between devices: 104 us -> 0 us
  Pallas kernels: 0 us -> 91.1 us
  blocking collectives: 82.5 us -> 0 us
  matrix products: 43.6 us -> 0 us
  between operations: 13.5 us -> 0.09 us
  other arithmetic: 12.3 us -> 0 us
    all_gather x2 -> x0, waiting for transfers between devices: 103 us -> none  [the longest x1 88.4 us: local(): lax.all_gather(w_o, CTX, axis=1, tiled=True)]
    pallas_call x0 -> x1, Pallas kernels: none -> 91.1 us  [local(): pl.pallas_call(kernel, out_shape=jax.ShapeDtypeStruct((TOK, NX * COLS), b...]
    all_gather x3 -> x0, blocking collectives: 56.4 us -> none  [gathered_by_axis(): array = lax.all_gather(array, axis, axis=dim, tiled=True)]
    dot_general x4 -> x0, matrix products: 43.6 us -> none  [the longest x1 11.9 us: local(): jnp.einsum('htl,lhv->thv', context, w_uv.reshape(LAT, heads, VDIM), prefe...]
    all_to_all x1 -> x0, blocking collectives: 26.1 us -> none  [sent_and_summed(): lax.all_to_all(parts, axis, split_axis=0, concat_axis=0, tiled=True)]
    reduce_sum x4 -> x0, other arithmetic: 11.9 us -> none  [the longest x1 9.28 us: local(): summed = jnp.sum(weight, axis=-1)]
    unnamed x3 -> x15, local copies, waits for them, and re-layouts: 1.03 us -> 5.26 us
  transfers between devices with their start and end apart: 2 -> 0, of which waited for: 2 -> 0; matrix products, arithmetic and copies ran while one was open for 18% -> 0% of each run, Pallas kernels for 0% -> 0%
where the time goes in v1:
time: 96.7 us; the launch traced here: 96.4 us
  Pallas kernels  91.1 us (94%)
  local copies, waits for them, and re-layouts  5.26 us (5%)
    pallas_call x1, Pallas kernels, local(): pl.pallas_call(kernel, out_shape=jax.ShapeDtypeStruct((TOK, NX * COLS), b...  91.1 us
    unnamed x15, local copies, waits for them, and re-layouts  5.26 us

profile of v1, /device:TPU:16, one launch (start us, length us, event | category | flops | bytes accessed | tf_op | source)
XLA Modules:
  0.0 96.4 jit_solution(9279072529334625258)
XLA Ops:
  0.0 0.8 copy.9.kr
  0.8 0.0 copy-start.2
  0.8 0.0 copy-start.3
  0.8 0.0 copy-start.4
  0.9 0.0 copy-start.5
  0.9 1.3 %copy.10.wo = bf16[1024,224]{1,0:T(8,128)(2,1)S(1)} copy(bf16[1024,224]{0,1:T(8,128)(2,1)} %param.15) | data formatting | bytes 917504 | tf_op args[7]
  2.2 0.0 copy-done.2
  2.2 0.0 copy-done.3
  2.2 0.0 copy-done.4
  2.2 0.0 copy-done.5
  2.2 0.0 copy-start
  2.2 1.2 %copy-done = bf16[512,1024]{1,0:T(8,128)(2,1)S(1)} copy-done((bf16[512,1024]{1,0:T(8,128)(2,1)S(1)}, bf16[512,1024]{1,0:T(8,128)(2,1)}, u32[]{:S(2)}) %copy-start) | copy-done | bytes 1048600
  3.4 0.0 copy-start.1
  3.4 1.2 %copy-done.1 = bf16[512,1024]{1,0:T(8,128)(2,1)S(1)} copy-done((bf16[512,1024]{1,0:T(8,128)(2,1)S(1)}, bf16[512,1024]{1,0:T(8,128)(2,1)}, u32[]{:S(2)}) %copy-start.1) | copy-done | bytes 1048600
  4.6 91.1 %shard_map.82 = bf16[128,896]{1,0:T(8,128)(2,1)S(1)} custom-call(bf16[128,1024]{1,0:T(8,128)(2,1)S(1)} %copy-done.2, bf16[128,512]{1,0:T(8,128)(2,1)S(1)} %copy-done.3, bf16[128,512]{1,0:T(8,128)(2,1)S(1)} %copy-done.4, bf16[128,64]{1,0:T(8,128)(2,1)S(1)} %copy.9.kr, s32[1,64]{1,0:T(1,128)S(1)} %bitcast.1, bf16[512,1024]{1,0:T(8,128)(2,1)S(1)} %copy-done, ...), custom_call_target="tpu_custom_call" | custom-call | flops 11000000512 | bytes 4000000 | tf_op jit(solution)/shard_map/pallas_call | solution.py:284
  95.7 0.7 copy.12
Async XLA Ops:
  0.8 1.3 %copy-start.2 = (bf16[128,1024]{1,0:T(8,128)(2,1)S(1)}, bf16[128,1024]{1,0:T(8,128)(2,1)}, u32[]{:S(2)}) copy-start(bf16[128,1024]{1,0:T(8,128)(2,1)} %qn.1) | copy-start | bytes 786436
  0.8 1.3 %copy-start.3 = (bf16[128,512]{1,0:T(8,128)(2,1)S(1)}, bf16[128,512]{1,0:T(8,128)(2,1)}, u32[]{:S(2)}) copy-start(bf16[128,512]{1,0:T(8,128)(2,1)} %qr.1) | copy-start | bytes 393220
  0.8 1.3 %copy-start.4 = (bf16[128,512]{1,0:T(8,128)(2,1)S(1)}, bf16[128,512]{1,0:T(8,128)(2,1)}, u32[]{:S(2)}) copy-start(bf16[128,512]{1,0:T(8,128)(2,1)} %lat.1) | copy-start | bytes 393220
  0.9 1.3 %copy-start.5 = (s32[64]{0:T(128)S(1)}, s32[64]{0:T(128)}, u32[]{:S(2)}) copy-start(s32[64]{0:T(128)} %param.12) | copy-start | bytes 772
  2.2 1.2 %copy-start = (bf16[512,1024]{1,0:T(8,128)(2,1)S(1)}, bf16[512,1024]{1,0:T(8,128)(2,1)}, u32[]{:S(2)}) copy-start(bf16[512,1024]{1,0:T(8,128)(2,1)} %wuk.1) | copy-start | bytes 3145732
  3.4 1.2 %copy-start.1 = (bf16[512,1024]{1,0:T(8,128)(2,1)S(1)}, bf16[512,1024]{1,0:T(8,128)(2,1)}, u32[]{:S(2)}) copy-start(bf16[512,1024]{1,0:T(8,128)(2,1)} %wuv.1) | copy-start | bytes 3145732

commit v2 on v0

v2 whole, which is shorter than its diff:
```python
import math

import jax
import jax.numpy as jnp
from jax import lax
from jax.experimental import pallas as pl
from jax.experimental.pallas import tpu as pltpu
from jax.sharding import Mesh
from jax.sharding import PartitionSpec as P

NZ, NX, NY = 8, 4, 4
TOK, SPAN, SPANS = 128, 64, 64
HEADS, NOPE, ROPE, LAT, VDIM = 8, 128, 64, 512, 128
WIDE = LAT + ROPE + SPANS
QUERIES = HEADS * TOK
COLS = 224
KEYS = NZ * NX * TOK
STRIP = TOK // (2 * NY)
BUNDLE = NZ * STRIP
CHUNK = 4 * BUNDLE
FACTOR = math.log2(math.e) / math.sqrt(NOPE + ROPE)
HIDDEN = -1e30
MESH = pl.DeviceIdType.MESH
DELTAS = (0, -1, 1, -2, 2, -3, 3, -4)


def nt_dot(a, b):
    return lax.dot_general(a, b, (((1,), (1,)), ((), ())), preferred_element_type=jnp.float32)


def tn_dot(a, b):
    return lax.dot_general(a, b, (((0,), (0,)), ((), ())), preferred_element_type=jnp.float32)


def nn_dot(a, b):
    return jnp.dot(a, b, preferred_element_type=jnp.float32)


def kernel(
    lat, kr, order, qn_in, qr_in, wuk_in, wuv_in, wo_in, out,
    qn, qr, wuk, wuv, kbuf, own_rope, qaug, acc, wuv_t, wbuf, hog, hog_t, c1s, c1r, c2s, c2r, c3s, c3r,
    in_sem, z_sem, w1_sem, w2_sem, p_sem, o_sem, a_sem, c1_sem, c2_sem, c3_sem,
):
    z, x, y, core = (lax.axis_index(n) for n in ("z", "x", "y", "core"))
    other = 1 - core

    def at(dz=0, dx=0, dy=0):
        return (lax.rem(z + NZ + dz, NZ), lax.rem(x + NX + dx, NX), lax.rem(y + NY + dy, NY), core)

    partner = (z, x, y, other)
    peers = [partner] + [at(dz=d) for d in range(1, NZ)]
    peers += [at(dx=d) for d in (1, 2, 3)] + [at(dy=d) for d in (1, 2, 3)]
    barrier = pltpu.get_barrier_semaphore()
    for peer in peers:
        pl.semaphore_signal(barrier, inc=1, device_id=peer, device_id_type=MESH)

    loads = []
    for n, (src, dst) in enumerate(
        ((wo_in, wbuf.at[z]), (wuk_in, wuk), (qn_in, qn), (qr_in, qr), (wuv_in, wuv))
    ):
        loads.append(pltpu.make_async_copy(src, dst, in_sem.at[n]))
        loads[-1].start()

    sent = []

    def copy(src, dst, sems, device):
        return pltpu.make_async_remote_copy(
            src_ref=src, dst_ref=dst, send_sem=sems[0], recv_sem=sems[1], device_id=device, device_id_type=MESH
        )

    def send(src, dst, sems, device):
        made = copy(src, dst, sems, device)
        made.start()
        sent.append(made)

    def arrived(dst, sems, device):
        copy(dst, dst, sems, device).wait_recv()

    def pair_of(sems, *index):
        return sems.at[(0, *index)], sems.at[(1, *index)]

    def base(k, a, b):
        first = x * (1 - k) + y * k + a + 4
        second = y * (1 - k) + x * k + b + 4
        return ((k * 4 + lax.rem(second, 4)) * 4 + lax.rem(first, 4)) * BUNDLE

    def bundle(k, a, b):
        return kbuf.at[pl.ds(pl.multiple_of(base(k, a, b), BUNDLE), BUNDLE)]

    def chunk(k, b):
        second = y * (1 - k) + x * k + b + 4
        return pl.ds(pl.multiple_of((k * 4 + lax.rem(second, 4)) * CHUNK, CHUNK), CHUNK)

    def along1(step):
        return at(dx=other * step, dy=core * step)

    def along2(step):
        return at(dx=core * step, dy=other * step)

    def strip(dz):
        start = base(core, 0, 0) + lax.rem(z + NZ + dz, NZ) * STRIP
        return pl.ds(pl.multiple_of(start, STRIP), STRIP)

    own_rope[...] = jnp.zeros_like(own_rope)
    own_rope[:, :ROPE] = kr[...].astype(jnp.float32).T.astype(jnp.bfloat16)
    mine = pl.ds(pl.multiple_of((2 * y + core) * STRIP, STRIP), STRIP)
    own_slot = (z * NX + x) * 2 + y // 2
    lane = lax.broadcasted_iota(jnp.int32, (STRIP, ROPE + SPANS), 1)
    kbuf[strip(0), :LAT] = lat[mine, :]
    kbuf[strip(0), LAT:] = jnp.where(
        lane == ROPE + own_slot, 1.0, own_rope[mine, :].astype(jnp.float32)
    ).astype(jnp.bfloat16)

    pl.semaphore_wait(barrier, len(peers))

    for d in (4, 3, 5, 2, 6, 1, 7):
        send(kbuf.at[strip(0)], kbuf.at[strip(0)], pair_of(z_sem, d), at(dz=d))

    tone = 1 - 2 * core
    ahead_z, behind_z = at(dz=tone), at(dz=-tone)

    def wpart(delta, half):
        zz = lax.rem(z + NZ + tone * delta, NZ)
        return wbuf.at[zz, pl.ds(half * (COLS // 2), COLS // 2)]

    def send_w(i, later, half):
        here = wpart(DELTAS[i], half)
        send(here, here, pair_of(o_sem, half, later), ahead_z if DELTAS[later] < 0 else behind_z)

    def wait_w(i, half):
        arrived(wpart(DELTAS[i], half), pair_of(o_sem, half, i), ahead_z if DELTAS[i] > 0 else behind_z)

    def serve_w(i, half):
        wait_w(i, half)
        if i + 2 < NZ:
            send_w(i, i + 2, half)

    loads[0].wait()
    for half in range(2):
        send_w(0, 1, half)
        send_w(0, 2, half)

    square = (SPANS, SPANS)
    places = order[...]
    diagonal = lax.broadcasted_iota(jnp.int32, square, 0) == lax.broadcasted_iota(jnp.int32, square, 1)
    column = jnp.sum(jnp.where(diagonal, jnp.broadcast_to(places, square), 0), axis=1, keepdims=True)
    slot_row = lax.broadcasted_iota(jnp.int32, (SPANS, TOK), 0)
    own_half = lax.broadcasted_iota(jnp.int32, (SPANS, TOK), 1) // SPAN
    own = slot_row == (z * NX + x) * 2 + own_half
    column = jnp.broadcast_to(column, (SPANS, TOK))
    place = jnp.sum(jnp.where(own, column, 0), axis=0, keepdims=True)
    mask = jnp.where(column >= place, HIDDEN, 0.0).astype(jnp.bfloat16)
    for n in (1, 2, 3):
        loads[n].wait()
    rot = qr[...].astype(jnp.float32).T.astype(jnp.bfloat16)
    for h in range(HEADS):
        cols = slice(h * TOK, (h + 1) * TOK)
        qaug[:LAT, cols] = nt_dot(wuk[:, cols], qn[:, cols]).astype(jnp.bfloat16)
        qaug[LAT : LAT + ROPE, cols] = rot[h * ROPE : (h + 1) * ROPE]
        qaug[LAT + ROPE :, cols] = mask

    def hand_on(a, first):
        here = bundle(core, a, 0)
        if first:
            for s in (2, 1, 3):
                send(here, here, pair_of(w1_sem, s), along1(s))
        for s in (2, 1, 3):
            send(here, here, pair_of(w2_sem, s, a), along2(s))
        send(here, here, pair_of(p_sem, 0, a), partner)

    def come(b):
        s = (4 - b) % 4
        for a in range(4):
            here = bundle(core, a, b)
            arrived(here, pair_of(w2_sem, s, a), along2(b))
            send(here, here, pair_of(p_sem, b, a), partner)

    def partner_has(b):
        for a in range(4):
            arrived(bundle(other, a, b), pair_of(p_sem, b, a), partner)

    def attend(spots, lo, size, top, total):
        cols = slice(lo, lo + size)
        scores = [nn_dot(kbuf[spot, :], qaug[:, cols]) * FACTOR for spot in spots]
        for spot, score in zip(spots, scores):
            newest = jnp.maximum(top, jnp.max(score, axis=0, keepdims=True))
            shrink = jnp.exp2(top - newest)
            weight = jnp.exp2(score - newest)
            total = total * shrink + jnp.sum(weight.reshape(CHUNK // 8, 8, size), axis=0)
            acc[:, cols] = acc[:, cols] * shrink + tn_dot(kbuf[spot, :LAT], weight.astype(jnp.bfloat16))
            top = newest
        return top, total

    for d in range(1, NZ):
        arrived(kbuf.at[strip(-d)], pair_of(z_sem, d), at(dz=-d))
    hand_on(0, True)

    row = lax.broadcasted_iota(jnp.int32, (TOK, QUERIES), 0)
    col = lax.rem(lax.broadcasted_iota(jnp.int32, (TOK, QUERIES), 1), TOK)
    seen = (row <= col) & (row >= (col // SPAN) * SPAN)
    score = nn_dot(lat[...], qaug[:LAT, :]) + nn_dot(own_rope[...], qaug[LAT:, :])
    score = jnp.where(seen, score * FACTOR, HIDDEN)
    top = jnp.max(score, axis=0, keepdims=True)
    weight = jnp.exp2(score - top)
    total = jnp.sum(weight.reshape(TOK // 8, 8, QUERIES), axis=0)
    acc[...] = tn_dot(lat[...], weight.astype(jnp.bfloat16))
    loads[4].wait()
    wuv_t[...] = wuv[...].T

    WING = QUERIES // 2
    state = [(top[:, n * WING : (n + 1) * WING], total[:, n * WING : (n + 1) * WING]) for n in range(2)]

    def attend_all(spot):
        for n in range(2):
            state[n] = attend([spot], n * WING, WING, *state[n])

    for a in (1, 3, 2):
        arrived(bundle(core, a, 0), pair_of(w1_sem, (4 - a) % 4), along1(a))
        hand_on(a, False)
    serve_w(1, 0)
    serve_w(2, 0)
    attend_all(chunk(core, 0))
    partner_has(0)
    attend_all(chunk(other, 0))
    serve_w(1, 1)
    serve_w(2, 1)
    come(1)
    attend_all(chunk(core, 1))
    come(3)
    attend_all(chunk(core, 3))
    serve_w(3, 0)
    serve_w(4, 0)
    partner_has(1)
    attend_all(chunk(other, 1))
    come(2)
    partner_has(3)
    attend_all(chunk(other, 3))
    attend_all(chunk(core, 2))
    serve_w(3, 1)
    serve_w(4, 1)
    partner_has(2)

    def send_heads(half, n):
        here = hog.at[half, x, :, n * WING : (n + 1) * WING]
        for d in (2, 1, 3):
            send(here, here, pair_of(a_sem, half, n, d), at(dx=d))

    for n in range(2):
        top, total = attend([chunk(other, 2)], n * WING, WING, *state[n])
        whole = jnp.sum(total, axis=0, keepdims=True)
        context = (acc[:, n * WING : (n + 1) * WING] / whole).astype(jnp.bfloat16)
        for k in range(HEADS // 2):
            spot = slice((n * HEADS // 2 + k) * VDIM, (n * HEADS // 2 + k + 1) * VDIM)
            done = nn_dot(wuv_t[spot, :], context[:, k * TOK : (k + 1) * TOK]).T.astype(jnp.bfloat16)
            for half in range(2):
                hog[half, x, :, spot] = done[half * SPAN : (half + 1) * SPAN]
        send_heads(0, n)
    for n in range(2):
        send_heads(1, n)
    for half in range(2):
        serve_w(5, half)
        serve_w(6, half)

    tilt = 1 - 2 * lax.rem(z, 2)
    order_y = [lax.rem(z // 2 + NY + step, NY) for step in (0, -tilt, tilt, 2)]
    ahead = []
    for half in range(2):
        for n in range(2):
            for d in (1, 2, 3):
                here = hog.at[half, lax.rem(x + NX - d, NX), :, n * WING : (n + 1) * WING]
                arrived(here, pair_of(a_sem, half, n, d), at(dx=-d))
        hog_t[...] = hog[half].reshape(NX * SPAN, HEADS * VDIM).T
        if half == 0:
            wait_w(7, 0)
            wait_w(7, 1)
        for n, j in enumerate(order_y):
            c1s[half, n] = nn_dot(wbuf[2 * j + other], hog_t[...]).astype(jnp.bfloat16)
            send(c1s.at[half, n], c1r.at[half, n], pair_of(c1_sem, half, n), partner)
        for n, j in enumerate(order_y):
            kept = nn_dot(wbuf[2 * j + core], hog_t[...])
            arrived(c1r.at[half, n], pair_of(c1_sem, half, n), partner)
            c2s[half, n] = (kept + c1r[half, n].astype(jnp.float32)).astype(jnp.bfloat16)
            sems = (c2_sem.at[0, half, n], c2_sem.at[1, half, y])
            onward = copy(c2s.at[half, n], c2r.at[half, y], sems, (z, x, j, core))
            ahead.append((j, onward))

            @pl.when(j != y)
            def _():
                onward.start()

            @pl.when(j == y)
            def _():
                c2r[half, y] = c2s[half, n]

    sums = []
    for half in range(2):
        for d in (1, 2, 3):
            yy = lax.rem(y + d, NY)
            arrived(c2r.at[half, yy], (c2_sem.at[0, half, 0], c2_sem.at[1, half, yy]), at(dy=d))
        summed = c2r[half, 0].astype(jnp.float32)
        for k in range(1, NY):
            summed = summed + c2r[half, k].astype(jnp.float32)
        sums.append(summed)
    for k in range(NX):
        both = [summed[:, k * SPAN : (k + 1) * SPAN] for summed in sums]
        c3s[k] = jnp.concatenate(both, axis=1).astype(jnp.bfloat16)
    for d in (2, 1, 3):
        send(c3s.at[lax.rem(x + d, NX)], c3r.at[x], pair_of(c3_sem, d), at(dx=d))
    c3r[x] = c3s[x]
    for d in (1, 2, 3):
        arrived(c3r.at[lax.rem(x + NX - d, NX)], pair_of(c3_sem, d), at(dx=-d))
    out[...] = c3r[...].reshape(NX * COLS, TOK).astype(jnp.float32).T.astype(jnp.bfloat16)

    for j, onward in ahead:

        @pl.when(j != y)
        def _():
            onward.wait_send()

    for made in sent:
        made.wait_send()


def local(q_nope, q_rope, latent, k_rope, span_order, w_uk, w_uv, w_o):
    bf16, f32 = jnp.bfloat16, jnp.float32
    dma = pltpu.SemaphoreType.DMA
    vmem = pl.BlockSpec(memory_space=pltpu.VMEM)
    anywhere = pl.BlockSpec(memory_space=pl.ANY)
    return pl.pallas_call(
        kernel,
        out_shape=jax.ShapeDtypeStruct((TOK, NX * COLS), bf16),
        in_specs=[vmem] * 3 + [anywhere] * 5,
        out_specs=vmem,
        scratch_shapes=[
            pltpu.VMEM((TOK, HEADS * NOPE), bf16),
            pltpu.VMEM((TOK, HEADS * ROPE), bf16),
            pltpu.VMEM((LAT, HEADS * NOPE), bf16),
            pltpu.VMEM((LAT, HEADS * VDIM), bf16),
            pltpu.VMEM((KEYS, WIDE), bf16),
            pltpu.VMEM((TOK, ROPE + SPANS), bf16),
            pltpu.VMEM((WIDE, QUERIES), bf16),
            pltpu.VMEM((LAT, QUERIES), f32),
            pltpu.VMEM((HEADS * VDIM, LAT), bf16),
            pltpu.VMEM((NZ, COLS, HEADS * VDIM), bf16),
            pltpu.VMEM((2, NX, SPAN, HEADS * VDIM), bf16),
            pltpu.VMEM((HEADS * VDIM, NX * SPAN), bf16),
            pltpu.VMEM((2, NY, COLS, NX * SPAN), bf16),
            pltpu.VMEM((2, NY, COLS, NX * SPAN), bf16),
            pltpu.VMEM((2, NY, COLS, NX * SPAN), bf16),
            pltpu.VMEM((2, NY, COLS, NX * SPAN), bf16),
            pltpu.VMEM((NX, COLS, TOK), bf16),
            pltpu.VMEM((NX, COLS, TOK), bf16),
            dma((5,)),
            dma((2, NZ)),
            dma((2, 4)),
            dma((2, 4, 4)),
            dma((2, 4, 4)),
            dma((2, 2, NZ)),
            dma((2, 2, 2, NX)),
            dma((2, 2, NY)),
            dma((2, 2, NY)),
            dma((2, NX)),
        ],
        compiler_params=pltpu.CompilerParams(
            collective_id=0, has_side_effects=True, vmem_limit_bytes=56 * 1024 * 1024
        ),
        cost_estimate=pl.CostEstimate(flops=11_000_000_000, bytes_accessed=4_000_000, transcendentals=4_200_000),
    )(latent, k_rope.T, span_order.reshape(1, -1), q_nope, q_rope, w_uk, w_uv, w_o.T)


def solution(mesh):
    torus = Mesh(mesh.devices.reshape(NZ, NX, NY, 2), ("z", "x", "y", "core"))
    ctx, head = ("z", "x"), ("y", "core")
    in_specs = (
        P(ctx, head),
        P(ctx, head),
        P(ctx, None),
        P(ctx, None),
        P(),
        P(None, head),
        P(None, head),
        P(head, ctx),
    )
    return jax.shard_map(local, mesh=torus, in_specs=in_specs, out_specs=P(ctx, head), check_vma=False)
```

time: 262 us -> 82.2 us (0.31)
  waiting for transfers between devices: 104 us -> 0 us
  blocking collectives: 82.5 us -> 0 us
  Pallas kernels: 0 us -> 79.3 us
  matrix products: 43.6 us -> 0 us
  between operations: 13.5 us -> 0.01 us
  other arithmetic: 12.3 us -> 0 us
    all_gather x2 -> x0, waiting for transfers between devices: 103 us -> none  [the longest x1 88.4 us: local(): lax.all_gather(w_o, CTX, axis=1, tiled=True)]
    pallas_call x0 -> x1, Pallas kernels: none -> 79.3 us  [local(): pl.pallas_call(kernel, out_shape=jax.ShapeDtypeStruct((TOK, NX * COLS), b...]
    all_gather x3 -> x0, blocking collectives: 56.4 us -> none  [gathered_by_axis(): array = lax.all_gather(array, axis, axis=dim, tiled=True)]
    dot_general x4 -> x0, matrix products: 43.6 us -> none  [the longest x1 11.9 us: local(): jnp.einsum('htl,lhv->thv', context, w_uv.reshape(LAT, heads, VDIM), prefe...]
    all_to_all x1 -> x0, blocking collectives: 26.1 us -> none  [sent_and_summed(): lax.all_to_all(parts, axis, split_axis=0, concat_axis=0, tiled=True)]
    reduce_sum x4 -> x0, other arithmetic: 11.9 us -> none  [the longest x1 9.28 us: local(): summed = jnp.sum(weight, axis=-1)]
  transfers between devices with their start and end apart: 2 -> 0, of which waited for: 2 -> 0; matrix products, arithmetic and copies ran while one was open for 18% -> 0% of each run, Pallas kernels for 0% -> 0%
where the time goes in v2:
time: 82.2 us; the launch traced here: 81 us
  Pallas kernels  79.3 us (96%)
  local copies, waits for them, and re-layouts  1.65 us (2%)
    pallas_call x1, Pallas kernels, local(): pl.pallas_call(kernel, out_shape=jax.ShapeDtypeStruct((TOK, NX * COLS), b...  79.3 us
    unnamed x1, local copies, waits for them, and re-layouts  1.65 us

profile of v2, /device:TPU:16, one launch (start us, length us, event | category | flops | bytes accessed | tf_op | source)
XLA Modules:
  0.0 81.0 jit_solution(5876875752388878254)
XLA Ops:
  0.0 79.3 %shard_map.82 = bf16[128,896]{1,0:T(8,128)(2,1)} custom-call(bf16[128,512]{1,0:T(8,128)(2,1)} %lat.1, bf16[64,128]{1,0:T(8,128)(2,1)} %bitcast.4, s32[1,64]{1,0:T(1,128)} %bitcast.5, bf16[128,1024]{1,0:T(8,128)(2,1)} %qn_in.1, bf16[128,512]{1,0:T(8,128)(2,1)} %qr_in.1, bf16[512,1024]{1,0:T(8,128)(2,1)} %wuk_in.1, bf16[512,1024]{1,0:T(8,128)(2,1)} %wuv_in.1, ...), custom_call_target="tpu_custom_call" | custom-call | flops 11000000512 | bytes 4000000 | tf_op jit(solution)/shard_map/pallas_call | solution.py:329
  79.3 1.6 %copy.10 = bf16[128,896]{1,0:T(8,128)(2,1)} copy(bf16[128,896]{1,0:T(8,128)(2,1)} %shard_map.82) | data formatting | bytes 458752

commit v3 on v2

--- a/solution.py
+++ b/solution.py
@@ -17,6 +17,8 @@
 KEYS = NZ * NX * TOK
 STRIP = TOK // (2 * NY)
 BUNDLE = NZ * STRIP
+GROUP = BUNDLE // 2
+PLACES = {0: 0, 1: 1, 7: 2, 2: 3, 6: 4, 3: 5, 5: 6, 4: 7}
 CHUNK = 4 * BUNDLE
 FACTOR = math.log2(math.e) / math.sqrt(NOPE + ROPE)
 HIDDEN = -1e30
@@ -38,7 +40,7 @@
 
 def kernel(
     lat, kr, order, qn_in, qr_in, wuk_in, wuv_in, wo_in, out,
-    qn, qr, wuk, wuv, kbuf, own_rope, qaug, acc, wuv_t, wbuf, hog, hog_t, c1s, c1r, c2s, c2r, c3s, c3r,
+    qn, qr, wuk, wuv, kbuf, own_rope, qaug, acc, wuv_t, wbuf, hog, c1s, c1r, c2s, c2r, c3s, c3r,
     in_sem, z_sem, w1_sem, w2_sem, p_sem, o_sem, a_sem, c1_sem, c2_sem, c3_sem,
 ):
     z, x, y, core = (lax.axis_index(n) for n in ("z", "x", "y", "core"))
@@ -87,6 +89,9 @@
     def bundle(k, a, b):
         return kbuf.at[pl.ds(pl.multiple_of(base(k, a, b), BUNDLE), BUNDLE)]
 
+    def group(a, b, n):
+        return kbuf.at[pl.ds(pl.multiple_of(base(core, a, b) + n * GROUP, GROUP), GROUP)]
+
     def chunk(k, b):
         second = y * (1 - k) + x * k + b + 4
         return pl.ds(pl.multiple_of((k * 4 + lax.rem(second, 4)) * CHUNK, CHUNK), CHUNK)
@@ -98,7 +103,7 @@
         return at(dx=core * step, dy=other * step)
 
     def strip(dz):
-        start = base(core, 0, 0) + lax.rem(z + NZ + dz, NZ) * STRIP
+        start = base(core, 0, 0) + PLACES[dz % NZ] * STRIP
         return pl.ds(pl.multiple_of(start, STRIP), STRIP)
 
     own_rope[...] = jnp.zeros_like(own_rope)
@@ -113,8 +118,8 @@
 
     pl.semaphore_wait(barrier, len(peers))
 
-    for d in (4, 3, 5, 2, 6, 1, 7):
-        send(kbuf.at[strip(0)], kbuf.at[strip(0)], pair_of(z_sem, d), at(dz=d))
+    for d in (6, 7, 1, 2, 4, 5, 3):
+        send(kbuf.at[strip(0)], kbuf.at[strip(-d)], pair_of(z_sem, d), at(dz=d))
 
     tone = 1 - 2 * core
     ahead_z, behind_z = at(dz=tone), at(dz=-tone)
@@ -159,21 +164,32 @@
         qaug[LAT : LAT + ROPE, cols] = rot[h * ROPE : (h + 1) * ROPE]
         qaug[LAT + ROPE :, cols] = mask
 
-    def hand_on(a, first):
-        here = bundle(core, a, 0)
-        if first:
+    def hand_on(a, n):
+        here = group(a, 0, n)
+        if a == 0:
             for s in (2, 1, 3):
-                send(here, here, pair_of(w1_sem, s), along1(s))
+                send(here, here, pair_of(w1_sem, n, s), along1(s))
         for s in (2, 1, 3):
-            send(here, here, pair_of(w2_sem, s, a), along2(s))
-        send(here, here, pair_of(p_sem, 0, a), partner)
+            send(here, here, pair_of(w2_sem, n, s, a), along2(s))
+        if n:
+            send(bundle(core, a, 0), bundle(core, a, 0), pair_of(p_sem, 0, a), partner)
+
+    def first_round(n):
+        for a in (1, 3, 2):
+            arrived(group(a, 0, n), pair_of(w1_sem, n, (4 - a) % 4), along1(a))
+            hand_on(a, n)
+
+    def from_z(n):
+        for d, place in PLACES.items():
+            if d and place // 4 == n:
+                arrived(kbuf.at[strip(d)], pair_of(z_sem, NZ - d), at(dz=d))
+        hand_on(0, n)
 
     def come(b):
-        s = (4 - b) % 4
-        for a in range(4):
-            here = bundle(core, a, b)
-            arrived(here, pair_of(w2_sem, s, a), along2(b))
-            send(here, here, pair_of(p_sem, b, a), partner)
+        for a in (0, 1, 3, 2):
+            for n in range(2):
+                arrived(group(a, b, n), pair_of(w2_sem, n, (4 - b) % 4, a), along2(b))
+            send(bundle(core, a, b), bundle(core, a, b), pair_of(p_sem, b, a), partner)
 
     def partner_has(b):
         for a in range(4):
@@ -191,9 +207,9 @@
             top = newest
         return top, total
 
-    for d in range(1, NZ):
-        arrived(kbuf.at[strip(-d)], pair_of(z_sem, d), at(dz=-d))
-    hand_on(0, True)
+    from_z(0)
+    from_z(1)
+    first_round(0)
 
     row = lax.broadcasted_iota(jnp.int32, (TOK, QUERIES), 0)
     col = lax.rem(lax.broadcasted_iota(jnp.int32, (TOK, QUERIES), 1), TOK)
@@ -214,9 +230,7 @@
         for n in range(2):
             state[n] = attend([spot], n * WING, WING, *state[n])
 
-    for a in (1, 3, 2):
-        arrived(bundle(core, a, 0), pair_of(w1_sem, (4 - a) % 4), along1(a))
-        hand_on(a, False)
+    first_round(1)
     serve_w(1, 0)
     serve_w(2, 0)
     attend_all(chunk(core, 0))
@@ -240,48 +254,40 @@
     serve_w(4, 1)
     partner_has(2)
 
-    def send_heads(half, n):
-        here = hog.at[half, x, :, n * WING : (n + 1) * WING]
-        for d in (2, 1, 3):
-            send(here, here, pair_of(a_sem, half, n, d), at(dx=d))
-
     for n in range(2):
+        half = slice(n * WING, (n + 1) * WING)
         top, total = attend([chunk(other, 2)], n * WING, WING, *state[n])
         whole = jnp.sum(total, axis=0, keepdims=True)
-        context = (acc[:, n * WING : (n + 1) * WING] / whole).astype(jnp.bfloat16)
+        context = (acc[:, half] / whole).astype(jnp.bfloat16)
         for k in range(HEADS // 2):
             spot = slice((n * HEADS // 2 + k) * VDIM, (n * HEADS // 2 + k + 1) * VDIM)
-            done = nn_dot(wuv_t[spot, :], context[:, k * TOK : (k + 1) * TOK]).T.astype(jnp.bfloat16)
-            for half in range(2):
-                hog[half, x, :, spot] = done[half * SPAN : (half + 1) * SPAN]
-        send_heads(0, n)
-    for n in range(2):
-        send_heads(1, n)
+            hog[x, spot] = nn_dot(wuv_t[spot, :], context[:, k * TOK : (k + 1) * TOK]).astype(jnp.bfloat16)
+        for d in (1, 3, 2):
+            send(hog.at[x, half], hog.at[x, half], pair_of(a_sem, n, d), at(dx=d))
     for half in range(2):
         serve_w(5, half)
         serve_w(6, half)
+    for half in range(2):
+        wait_w(7, half)
 
     tilt = 1 - 2 * lax.rem(z, 2)
     order_y = [lax.rem(z // 2 + NY + step, NY) for step in (0, -tilt, tilt, 2)]
     ahead = []
-    for half in range(2):
-        for n in range(2):
-            for d in (1, 2, 3):
-                here = hog.at[half, lax.rem(x + NX - d, NX), :, n * WING : (n + 1) * WING]
-                arrived(here, pair_of(a_sem, half, n, d), at(dx=-d))
-        hog_t[...] = hog[half].reshape(NX * SPAN, HEADS * VDIM).T
-        if half == 0:
-            wait_w(7, 0)
-            wait_w(7, 1)
+
+    def project(o):
+        block = lax.rem(x + o, NX)
+        if o:
+            for n in range(2):
+                arrived(hog.at[block, n * WING : (n + 1) * WING], pair_of(a_sem, n, NX - o), at(dx=o))
         for n, j in enumerate(order_y):
-            c1s[half, n] = nn_dot(wbuf[2 * j + other], hog_t[...]).astype(jnp.bfloat16)
-            send(c1s.at[half, n], c1r.at[half, n], pair_of(c1_sem, half, n), partner)
+            c1s[o, n] = nn_dot(wbuf[2 * j + other], hog[block]).astype(jnp.bfloat16)
+            send(c1s.at[o, n], c1r.at[o, n], pair_of(c1_sem, o, n), partner)
         for n, j in enumerate(order_y):
-            kept = nn_dot(wbuf[2 * j + core], hog_t[...])
-            arrived(c1r.at[half, n], pair_of(c1_sem, half, n), partner)
-            c2s[half, n] = (kept + c1r[half, n].astype(jnp.float32)).astype(jnp.bfloat16)
-            sems = (c2_sem.at[0, half, n], c2_sem.at[1, half, y])
-            onward = copy(c2s.at[half, n], c2r.at[half, y], sems, (z, x, j, core))
+            kept = nn_dot(wbuf[2 * j + core], hog[block])
+            arrived(c1r.at[o, n], pair_of(c1_sem, o, n), partner)
+            c2s[o, n] = (kept + c1r[o, n].astype(jnp.float32)).astype(jnp.bfloat16)
+            sems = (c2_sem.at[0, o, n], c2_sem.at[1, o, y])
+            onward = copy(c2s.at[o, n], c2r.at[o, y], sems, (z, x, j, core))
             ahead.append((j, onward))
 
             @pl.when(j != y)
@@ -290,23 +296,29 @@
 
             @pl.when(j == y)
             def _():
-                c2r[half, y] = c2s[half, n]
-
-    sums = []
-    for half in range(2):
+                c2r[o, y] = c2s[o, n]
+
+    def collect(o):
         for d in (1, 2, 3):
             yy = lax.rem(y + d, NY)
-            arrived(c2r.at[half, yy], (c2_sem.at[0, half, 0], c2_sem.at[1, half, yy]), at(dy=d))
-        summed = c2r[half, 0].astype(jnp.float32)
+            arrived(c2r.at[o, yy], (c2_sem.at[0, o, 0], c2_sem.at[1, o, yy]), at(dy=d))
+        summed = c2r[o, 0].astype(jnp.float32)
         for k in range(1, NY):
-            summed = summed + c2r[half, k].astype(jnp.float32)
-        sums.append(summed)
-    for k in range(NX):
-        both = [summed[:, k * SPAN : (k + 1) * SPAN] for summed in sums]
-        c3s[k] = jnp.concatenate(both, axis=1).astype(jnp.bfloat16)
-    for d in (2, 1, 3):
-        send(c3s.at[lax.rem(x + d, NX)], c3r.at[x], pair_of(c3_sem, d), at(dx=d))
-    c3r[x] = c3s[x]
+            summed = summed + c2r[o, k].astype(jnp.float32)
+        if o:
+            c3s[o] = summed.astype(jnp.bfloat16)
+            send(c3s.at[o], c3r.at[x], pair_of(c3_sem, o), at(dx=o))
+        else:
+            c3r[x] = summed.astype(jnp.bfloat16)
+
+    project(0)
+    project(1)
+    collect(0)
+    project(3)
+    collect(1)
+    project(2)
+    collect(3)
+    collect(2)
     for d in (1, 2, 3):
         arrived(c3r.at[lax.rem(x + NX - d, NX)], pair_of(c3_sem, d), at(dx=-d))
     out[...] = c3r[...].reshape(NX * COLS, TOK).astype(jnp.float32).T.astype(jnp.bfloat16)
@@ -342,23 +354,22 @@
             pltpu.VMEM((LAT, QUERIES), f32),
             pltpu.VMEM((HEADS * VDIM, LAT), bf16),
             pltpu.VMEM((NZ, COLS, HEADS * VDIM), bf16),
-            pltpu.VMEM((2, NX, SPAN, HEADS * VDIM), bf16),
-            pltpu.VMEM((HEADS * VDIM, NX * SPAN), bf16),
-            pltpu.VMEM((2, NY, COLS, NX * SPAN), bf16),
-            pltpu.VMEM((2, NY, COLS, NX * SPAN), bf16),
-            pltpu.VMEM((2, NY, COLS, NX * SPAN), bf16),
-            pltpu.VMEM((2, NY, COLS, NX * SPAN), bf16),
+            pltpu.VMEM((NX, HEADS * VDIM, TOK), bf16),
+            pltpu.VMEM((NX, NY, COLS, TOK), bf16),
+            pltpu.VMEM((NX, NY, COLS, TOK), bf16),
+            pltpu.VMEM((NX, NY, COLS, TOK), bf16),
+            pltpu.VMEM((NX, NY, COLS, TOK), bf16),
             pltpu.VMEM((NX, COLS, TOK), bf16),
             pltpu.VMEM((NX, COLS, TOK), bf16),
             dma((5,)),
             dma((2, NZ)),
-            dma((2, 4)),
-            dma((2, 4, 4)),
+            dma((2, 2, 4)),
+            dma((2, 2, 4, 4)),
             dma((2, 4, 4)),
             dma((2, 2, NZ)),
-            dma((2, 2, 2, NX)),
-            dma((2, 2, NY)),
-            dma((2, 2, NY)),
+            dma((2, 2, NX)),
+            dma((2, NX, NY)),
+            dma((2, NX, NY)),
             dma((2, NX)),
         ],
         compiler_params=pltpu.CompilerParams(

time: 82.2 us -> 81.3 us (0.989); the launches traced: 81 us -> 81.1 us
  no operation moved by 1% of the time
where the time goes in v3:
time: 81.3 us; the launch traced here: 81.1 us
  Pallas kernels  79.5 us (98%)
  local copies, waits for them, and re-layouts  1.65 us (2%)
    pallas_call x1, Pallas kernels, local(): pl.pallas_call(kernel, out_shape=jax.ShapeDtypeStruct((TOK, NX * COLS), b...  79.5 us
    unnamed x1, local copies, waits for them, and re-layouts  1.65 us

profile of v3, /device:TPU:16, one launch (start us, length us, event | category | flops | bytes accessed | tf_op | source)
XLA Modules:
  0.0 81.1 jit_solution(17388890536598633960)
XLA Ops:
  0.0 79.5 %shard_map.82 = bf16[128,896]{1,0:T(8,128)(2,1)} custom-call(bf16[128,512]{1,0:T(8,128)(2,1)} %lat.1, bf16[64,128]{1,0:T(8,128)(2,1)} %bitcast.4, s32[1,64]{1,0:T(1,128)} %bitcast.5, bf16[128,1024]{1,0:T(8,128)(2,1)} %qn_in.1, bf16[128,512]{1,0:T(8,128)(2,1)} %qr_in.1, bf16[512,1024]{1,0:T(8,128)(2,1)} %wuk_in.1, bf16[512,1024]{1,0:T(8,128)(2,1)} %wuv_in.1, ...), custom_call_target="tpu_custom_call" | custom-call | flops 11000000512 | bytes 4000000 | tf_op jit(solution)/shard_map/pallas_call | solution.py:341
  79.5 1.6 %copy.10 = bf16[128,896]{1,0:T(8,128)(2,1)} copy(bf16[128,896]{1,0:T(8,128)(2,1)} %shard_map.82) | data formatting | bytes 458752

commit v4 on v3

--- a/solution.py
+++ b/solution.py
@@ -81,29 +81,32 @@
     def pair_of(sems, *index):
         return sems.at[(0, *index)], sems.at[(1, *index)]
 
-    def base(k, a, b):
-        first = x * (1 - k) + y * k + a + 4
-        second = y * (1 - k) + x * k + b + 4
-        return ((k * 4 + lax.rem(second, 4)) * 4 + lax.rem(first, 4)) * BUNDLE
-
-    def bundle(k, a, b):
-        return kbuf.at[pl.ds(pl.multiple_of(base(k, a, b), BUNDLE), BUNDLE)]
-
-    def group(a, b, n):
-        return kbuf.at[pl.ds(pl.multiple_of(base(core, a, b) + n * GROUP, GROUP), GROUP)]
-
-    def chunk(k, b):
-        second = y * (1 - k) + x * k + b + 4
-        return pl.ds(pl.multiple_of((k * 4 + lax.rem(second, 4)) * CHUNK, CHUNK), CHUNK)
-
-    def along1(step):
-        return at(dx=other * step, dy=core * step)
-
-    def along2(step):
-        return at(dx=core * step, dy=other * step)
+    def chunk_start(n, b):
+        second = (x if n else y) + b + 4
+        return (n * 4 + lax.rem(second, 4)) * CHUNK
+
+    def chunk(n, b):
+        return pl.ds(pl.multiple_of(chunk_start(n, b), CHUNK), CHUNK)
+
+    def share(k, n, b):
+        return kbuf.at[pl.ds(pl.multiple_of(chunk_start(n, b) + k * (CHUNK // 2), CHUNK // 2), CHUNK // 2)]
+
+    def group_start(n, a, b):
+        first = (y if n else x) + a + 4
+        return chunk_start(n, b) + core * (CHUNK // 2) + lax.rem(first, 4) * GROUP
+
+    def group(n, a, b):
+        return kbuf.at[pl.ds(pl.multiple_of(group_start(n, a, b), GROUP), GROUP)]
+
+    def along1(n, step):
+        return at(dy=step) if n else at(dx=step)
+
+    def along2(n, step):
+        return at(dx=step) if n else at(dy=step)
 
     def strip(dz):
-        start = base(core, 0, 0) + PLACES[dz % NZ] * STRIP
+        place = PLACES[dz % NZ]
+        start = group_start(place // 4, 0, 0) + place % 4 * STRIP
         return pl.ds(pl.multiple_of(start, STRIP), STRIP)
 
     own_rope[...] = jnp.zeros_like(own_rope)
@@ -164,36 +167,36 @@
         qaug[LAT : LAT + ROPE, cols] = rot[h * ROPE : (h + 1) * ROPE]
         qaug[LAT + ROPE :, cols] = mask
 
-    def hand_on(a, n):
-        here = group(a, 0, n)
+    def hand_on(n, a):
+        here = group(n, a, 0)
         if a == 0:
-            for s in (2, 1, 3):
-                send(here, here, pair_of(w1_sem, n, s), along1(s))
-        for s in (2, 1, 3):
-            send(here, here, pair_of(w2_sem, n, s, a), along2(s))
-        if n:
-            send(bundle(core, a, 0), bundle(core, a, 0), pair_of(p_sem, 0, a), partner)
-
-    def first_round(n):
-        for a in (1, 3, 2):
-            arrived(group(a, 0, n), pair_of(w1_sem, n, (4 - a) % 4), along1(a))
-            hand_on(a, n)
+            for s in (1, 3, 2):
+                send(here, here, pair_of(w1_sem, n, s), along1(n, s))
+        for s in (1, 3):
+            send(here, here, pair_of(w2_sem, n, s, a), along2(n, s))
 
     def from_z(n):
         for d, place in PLACES.items():
             if d and place // 4 == n:
                 arrived(kbuf.at[strip(d)], pair_of(z_sem, NZ - d), at(dz=d))
-        hand_on(0, n)
-
-    def come(b):
+        hand_on(n, 0)
+
+    def first_round(n):
+        for a in (1, 3, 2):
+            arrived(group(n, a, 0), pair_of(w1_sem, n, 4 - a), along1(n, a))
+            hand_on(n, a)
+        send(share(core, n, 0), share(core, n, 0), pair_of(p_sem, n, 0), partner)
+
+    def come(n, b):
         for a in (0, 1, 3, 2):
-            for n in range(2):
-                arrived(group(a, b, n), pair_of(w2_sem, n, (4 - b) % 4, a), along2(b))
-            send(bundle(core, a, b), bundle(core, a, b), pair_of(p_sem, b, a), partner)
-
-    def partner_has(b):
-        for a in range(4):
-            arrived(bundle(other, a, b), pair_of(p_sem, b, a), partner)
+            here = group(n, a, b)
+            arrived(here, pair_of(w2_sem, n, 4 - b, a), along2(n, b))
+            if (b, a) in ((1, 0), (1, 1), (3, 2), (3, 3)):
+                send(here, here, pair_of(w2_sem, n, 2, a), along2(n, -b if b == 1 else 1))
+        send(share(core, n, b), share(core, n, b), pair_of(p_sem, n, b), partner)
+
+    def partner_has(n, b):
+        arrived(share(other, n, b), pair_of(p_sem, n, b), partner)
 
     def attend(spots, lo, size, top, total):
         cols = slice(lo, lo + size)
@@ -208,8 +211,9 @@
         return top, total
 
     from_z(0)
+    first_round(0)
     from_z(1)
-    first_round(0)
+    first_round(1)
 
     row = lax.broadcasted_iota(jnp.int32, (TOK, QUERIES), 0)
     col = lax.rem(lax.broadcasted_iota(jnp.int32, (TOK, QUERIES), 1), TOK)
@@ -226,47 +230,57 @@
     WING = QUERIES // 2
     state = [(top[:, n * WING : (n + 1) * WING], total[:, n * WING : (n + 1) * WING]) for n in range(2)]
 
-    def attend_all(spot):
+    def attend_all(n, b):
+        partner_has(n, b)
+        spot = chunk(n, b)
         for n in range(2):
             state[n] = attend([spot], n * WING, WING, *state[n])
 
-    first_round(1)
-    serve_w(1, 0)
-    serve_w(2, 0)
-    attend_all(chunk(core, 0))
-    partner_has(0)
-    attend_all(chunk(other, 0))
-    serve_w(1, 1)
-    serve_w(2, 1)
-    come(1)
-    attend_all(chunk(core, 1))
-    come(3)
-    attend_all(chunk(core, 3))
-    serve_w(3, 0)
-    serve_w(4, 0)
-    partner_has(1)
-    attend_all(chunk(other, 1))
-    come(2)
-    partner_has(3)
-    attend_all(chunk(other, 3))
-    attend_all(chunk(core, 2))
-    serve_w(3, 1)
-    serve_w(4, 1)
-    partner_has(2)
+    def serve(step, half):
+        serve_w(2 * step - 1, half)
+        serve_w(2 * step, half)
+
+    serve(1, 0)
+    attend_all(0, 0)
+    come(0, 1)
+    come(0, 3)
+    attend_all(1, 0)
+    come(1, 1)
+    come(1, 3)
+    serve(1, 1)
+    attend_all(0, 1)
+    come(0, 2)
+    serve(2, 0)
+    attend_all(0, 3)
+    come(1, 2)
+    attend_all(1, 1)
+    serve(2, 1)
+    attend_all(1, 3)
+    attend_all(0, 2)
+    serve(3, 0)
+    partner_has(1, 2)
 
     for n in range(2):
         half = slice(n * WING, (n + 1) * WING)
-        top, total = attend([chunk(other, 2)], n * WING, WING, *state[n])
+        top, total = attend([chunk(1, 2)], n * WING, WING, *state[n])
         whole = jnp.sum(total, axis=0, keepdims=True)
         context = (acc[:, half] / whole).astype(jnp.bfloat16)
         for k in range(HEADS // 2):
             spot = slice((n * HEADS // 2 + k) * VDIM, (n * HEADS // 2 + k + 1) * VDIM)
             hog[x, spot] = nn_dot(wuv_t[spot, :], context[:, k * TOK : (k + 1) * TOK]).astype(jnp.bfloat16)
-        for d in (1, 3, 2):
+        for d in (1, 3):
             send(hog.at[x, half], hog.at[x, half], pair_of(a_sem, n, d), at(dx=d))
-    for half in range(2):
-        serve_w(5, half)
-        serve_w(6, half)
+    serve(3, 1)
+
+    def heads_from(n, o):
+        here = hog.at[lax.rem(x + o, NX), n * WING : (n + 1) * WING]
+        arrived(here, pair_of(a_sem, n, NX - o), at(dx=o))
+        return here
+
+    passed = heads_from(0, 1)
+    send(passed, passed, pair_of(a_sem, 0, 2), at(dx=-1))
+    passed = heads_from(1, 3)
+    send(passed, passed, pair_of(a_sem, 1, 2), at(dx=1))
     for half in range(2):
         wait_w(7, half)
 
@@ -276,9 +290,8 @@
 
     def project(o):
         block = lax.rem(x + o, NX)
-        if o:
-            for n in range(2):
-                arrived(hog.at[block, n * WING : (n + 1) * WING], pair_of(a_sem, n, NX - o), at(dx=o))
+        for n in {1: (1,), 2: (0, 1), 3: (0,)}.get(o, ()):
+            heads_from(n, o)
         for n, j in enumerate(order_y):
             c1s[o, n] = nn_dot(wbuf[2 * j + other], hog[block]).astype(jnp.bfloat16)
             send(c1s.at[o, n], c1r.at[o, n], pair_of(c1_sem, o, n), partner)
@@ -365,7 +378,7 @@
             dma((2, NZ)),
             dma((2, 2, 4)),
             dma((2, 2, 4, 4)),
-            dma((2, 4, 4)),
+            dma((2, 2, 4)),
             dma((2, 2, NZ)),
             dma((2, 2, NX)),
             dma((2, NX, NY)),

time: 81.3 us -> 80.1 us (0.985)
  Pallas kernels: 79.5 us -> 77.5 us
    pallas_call x1, Pallas kernels: 79.5 us -> 77.5 us  [local(): pl.pallas_call(kernel, out_shape=jax.ShapeDtypeStruct((TOK, NX * COLS), b...]
where the time goes in v4:
time: 80.1 us; the launch traced here: 79.1 us
  Pallas kernels  77.5 us (97%)
  local copies, waits for them, and re-layouts  1.65 us (2%)
    pallas_call x1, Pallas kernels, local(): pl.pallas_call(kernel, out_shape=jax.ShapeDtypeStruct((TOK, NX * COLS), b...  77.5 us
    unnamed x1, local copies, waits for them, and re-layouts  1.65 us

profile of v4, /device:TPU:16, one launch (start us, length us, event | category | flops | bytes accessed | tf_op | source)
XLA Modules:
  0.0 79.1 jit_solution(74303955763516273)
XLA Ops:
  0.0 77.5 %shard_map.82 = bf16[128,896]{1,0:T(8,128)(2,1)} custom-call(bf16[128,512]{1,0:T(8,128)(2,1)} %lat.1, bf16[64,128]{1,0:T(8,128)(2,1)} %bitcast.4, s32[1,64]{1,0:T(1,128)} %bitcast.5, bf16[128,1024]{1,0:T(8,128)(2,1)} %qn_in.1, bf16[128,512]{1,0:T(8,128)(2,1)} %qr_in.1, bf16[512,1024]{1,0:T(8,128)(2,1)} %wuk_in.1, bf16[512,1024]{1,0:T(8,128)(2,1)} %wuv_in.1, ...), custom_call_target="tpu_custom_call" | custom-call | flops 11000000512 | bytes 4000000 | tf_op jit(solution)/shard_map/pallas_call | solution.py:354
  77.5 1.6 %copy.10 = bf16[128,896]{1,0:T(8,128)(2,1)} copy(bf16[128,896]{1,0:T(8,128)(2,1)} %shard_map.82) | data formatting | bytes 458752

commit v5 on v4

--- a/solution.py
+++ b/solution.py
@@ -119,11 +119,6 @@
         lane == ROPE + own_slot, 1.0, own_rope[mine, :].astype(jnp.float32)
     ).astype(jnp.bfloat16)
 
-    pl.semaphore_wait(barrier, len(peers))
-
-    for d in (6, 7, 1, 2, 4, 5, 3):
-        send(kbuf.at[strip(0)], kbuf.at[strip(-d)], pair_of(z_sem, d), at(dz=d))
-
     tone = 1 - 2 * core
     ahead_z, behind_z = at(dz=tone), at(dz=-tone)
 
@@ -142,11 +137,6 @@
         wait_w(i, half)
         if i + 2 < NZ:
             send_w(i, i + 2, half)
-
-    loads[0].wait()
-    for half in range(2):
-        send_w(0, 1, half)
-        send_w(0, 2, half)
 
     square = (SPANS, SPANS)
     places = order[...]
@@ -167,6 +157,28 @@
         qaug[LAT : LAT + ROPE, cols] = rot[h * ROPE : (h + 1) * ROPE]
         qaug[LAT + ROPE :, cols] = mask
 
+    pl.semaphore_wait(barrier, len(peers))
+
+    for d in (6, 7, 1, 2, 4, 5, 3):
+        send(kbuf.at[strip(0)], kbuf.at[strip(-d)], pair_of(z_sem, d), at(dz=d))
+
+    loads[0].wait()
+    for half in range(2):
+        for later in (1, 2):
+            send_w(0, later, half)
+
+    row = lax.broadcasted_iota(jnp.int32, (TOK, QUERIES), 0)
+    col = lax.rem(lax.broadcasted_iota(jnp.int32, (TOK, QUERIES), 1), TOK)
+    seen = (row <= col) & (row >= (col // SPAN) * SPAN)
+    score = nn_dot(lat[...], qaug[:LAT, :]) + nn_dot(own_rope[...], qaug[LAT:, :])
+    score = jnp.where(seen, score * FACTOR, HIDDEN)
+    top = jnp.max(score, axis=0, keepdims=True)
+    weight = jnp.exp2(score - top)
+    total = jnp.sum(weight.reshape(TOK // 8, 8, QUERIES), axis=0)
+    acc[...] = tn_dot(lat[...], weight.astype(jnp.bfloat16))
+    loads[4].wait()
+    wuv_t[...] = wuv[...].T
+
     def hand_on(n, a):
         here = group(n, a, 0)
         if a == 0:
@@ -215,18 +227,6 @@
     from_z(1)
     first_round(1)
 
-    row = lax.broadcasted_iota(jnp.int32, (TOK, QUERIES), 0)
-    col = lax.rem(lax.broadcasted_iota(jnp.int32, (TOK, QUERIES), 1), TOK)
-    seen = (row <= col) & (row >= (col // SPAN) * SPAN)
-    score = nn_dot(lat[...], qaug[:LAT, :]) + nn_dot(own_rope[...], qaug[LAT:, :])
-    score = jnp.where(seen, score * FACTOR, HIDDEN)
-    top = jnp.max(score, axis=0, keepdims=True)
-    weight = jnp.exp2(score - top)
-    total = jnp.sum(weight.reshape(TOK // 8, 8, QUERIES), axis=0)
-    acc[...] = tn_dot(lat[...], weight.astype(jnp.bfloat16))
-    loads[4].wait()
-    wuv_t[...] = wuv[...].T
-
     WING = QUERIES // 2
     state = [(top[:, n * WING : (n + 1) * WING], total[:, n * WING : (n + 1) * WING]) for n in range(2)]
 
@@ -242,22 +242,23 @@
 
     serve(1, 0)
     attend_all(0, 0)
+    serve(1, 1)
     come(0, 1)
     come(0, 3)
     attend_all(1, 0)
+    serve(2, 0)
     come(1, 1)
     come(1, 3)
-    serve(1, 1)
+    serve(2, 1)
     attend_all(0, 1)
     come(0, 2)
-    serve(2, 0)
+    serve(3, 0)
     attend_all(0, 3)
     come(1, 2)
     attend_all(1, 1)
-    serve(2, 1)
+    serve(3, 1)
     attend_all(1, 3)
     attend_all(0, 2)
-    serve(3, 0)
     partner_has(1, 2)
 
     for n in range(2):
@@ -270,17 +271,19 @@
             hog[x, spot] = nn_dot(wuv_t[spot, :], context[:, k * TOK : (k + 1) * TOK]).astype(jnp.bfloat16)
         for d in (1, 3):
             send(hog.at[x, half], hog.at[x, half], pair_of(a_sem, n, d), at(dx=d))
-    serve(3, 1)
 
     def heads_from(n, o):
         here = hog.at[lax.rem(x + o, NX), n * WING : (n + 1) * WING]
         arrived(here, pair_of(a_sem, n, NX - o), at(dx=o))
         return here
 
+    early = list(sent)
+    sent.clear()
+
     passed = heads_from(0, 1)
     send(passed, passed, pair_of(a_sem, 0, 2), at(dx=-1))
-    passed = heads_from(1, 3)
-    send(passed, passed, pair_of(a_sem, 1, 2), at(dx=1))
+    for made in early:
+        made.wait_send()
     for half in range(2):
         wait_w(7, half)
 
@@ -288,28 +291,30 @@
     order_y = [lax.rem(z // 2 + NY + step, NY) for step in (0, -tilt, tilt, 2)]
     ahead = []
 
-    def project(o):
-        block = lax.rem(x + o, NX)
-        for n in {1: (1,), 2: (0, 1), 3: (0,)}.get(o, ()):
-            heads_from(n, o)
+    def project(*steps):
+        right = jnp.concatenate([hog[lax.rem(x + o, NX)] for o in steps], axis=1)
+        parts = [(o, slice(i * TOK, (i + 1) * TOK)) for i, o in enumerate(steps)]
         for n, j in enumerate(order_y):
-            c1s[o, n] = nn_dot(wbuf[2 * j + other], hog[block]).astype(jnp.bfloat16)
-            send(c1s.at[o, n], c1r.at[o, n], pair_of(c1_sem, o, n), partner)
+            given = nn_dot(wbuf[2 * j + other], right).astype(jnp.bfloat16)
+            for o, part in parts:
+                c1s[o, n] = given[:, part]
+                send(c1s.at[o, n], c1r.at[o, n], pair_of(c1_sem, o, n), partner)
         for n, j in enumerate(order_y):
-            kept = nn_dot(wbuf[2 * j + core], hog[block])
-            arrived(c1r.at[o, n], pair_of(c1_sem, o, n), partner)
-            c2s[o, n] = (kept + c1r[o, n].astype(jnp.float32)).astype(jnp.bfloat16)
-            sems = (c2_sem.at[0, o, n], c2_sem.at[1, o, y])
-            onward = copy(c2s.at[o, n], c2r.at[o, y], sems, (z, x, j, core))
-            ahead.append((j, onward))
-
-            @pl.when(j != y)
-            def _():
-                onward.start()
-
-            @pl.when(j == y)
-            def _():
-                c2r[o, y] = c2s[o, n]
+            kept = nn_dot(wbuf[2 * j + core], right)
+            for o, part in parts:
+                arrived(c1r.at[o, n], pair_of(c1_sem, o, n), partner)
+                c2s[o, n] = (kept[:, part] + c1r[o, n].astype(jnp.float32)).astype(jnp.bfloat16)
+                sems = (c2_sem.at[0, o, n], c2_sem.at[1, o, y])
+                onward = copy(c2s.at[o, n], c2r.at[o, y], sems, (z, x, j, core))
+                ahead.append((j, onward))
+
+                @pl.when(j != y)
+                def _():
+                    onward.start()
+
+                @pl.when(j == y)
+                def _():
+                    c2r[o, y] = c2s[o, n]
 
     def collect(o):
         for d in (1, 2, 3):
@@ -325,11 +330,16 @@
             c3r[x] = summed.astype(jnp.bfloat16)
 
     project(0)
-    project(1)
+    passed = heads_from(1, 3)
+    send(passed, passed, pair_of(a_sem, 1, 2), at(dx=1))
+    heads_from(1, 1)
+    heads_from(0, 3)
+    project(1, 3)
     collect(0)
-    project(3)
+    heads_from(0, 2)
+    heads_from(1, 2)
+    project(2)
     collect(1)
-    project(2)
     collect(3)
     collect(2)
     for d in (1, 2, 3):

time: 80.1 us -> 81.9 us (1.022); the launches traced: 79.1 us -> 81.8 us
  Pallas kernels: 77.5 us -> 80.1 us
    pallas_call x1, Pallas kernels: 77.5 us -> 80.1 us  [local(): pl.pallas_call(kernel, out_shape=jax.ShapeDtypeStruct((TOK, NX * COLS), b...]
where the time goes in v5:
time: 81.9 us; the launch traced here: 81.8 us
  Pallas kernels  80.1 us (98%)
  local copies, waits for them, and re-layouts  1.65 us (2%)
    pallas_call x1, Pallas kernels, local(): pl.pallas_call(kernel, out_shape=jax.ShapeDtypeStruct((TOK, NX * COLS), b...  80.1 us
    unnamed x1, local copies, waits for them, and re-layouts  1.65 us

profile of v5, /device:TPU:16, one launch (start us, length us, event | category | flops | bytes accessed | tf_op | source)
XLA Modules:
  0.0 81.8 jit_solution(3543972477790821588)
XLA Ops:
  0.0 80.1 %shard_map.82 = bf16[128,896]{1,0:T(8,128)(2,1)} custom-call(bf16[128,512]{1,0:T(8,128)(2,1)} %lat.1, bf16[64,128]{1,0:T(8,128)(2,1)} %bitcast.4, s32[1,64]{1,0:T(1,128)} %bitcast.5, bf16[128,1024]{1,0:T(8,128)(2,1)} %qn_in.1, bf16[128,512]{1,0:T(8,128)(2,1)} %qr_in.1, bf16[512,1024]{1,0:T(8,128)(2,1)} %wuk_in.1, bf16[512,1024]{1,0:T(8,128)(2,1)} %wuv_in.1, ...), custom_call_target="tpu_custom_call" | custom-call | flops 11000000512 | bytes 4000000 | tf_op jit(solution)/shard_map/pallas_call | solution.py:364
  80.2 1.6 %copy.10 = bf16[128,896]{1,0:T(8,128)(2,1)} copy(bf16[128,896]{1,0:T(8,128)(2,1)} %shard_map.82) | data formatting | bytes 458752

commit v6 on v4

--- a/solution.py
+++ b/solution.py
@@ -288,28 +288,30 @@
     order_y = [lax.rem(z // 2 + NY + step, NY) for step in (0, -tilt, tilt, 2)]
     ahead = []
 
-    def project(o):
-        block = lax.rem(x + o, NX)
-        for n in {1: (1,), 2: (0, 1), 3: (0,)}.get(o, ()):
-            heads_from(n, o)
+    def project(*steps):
+        right = jnp.concatenate([hog[lax.rem(x + o, NX)] for o in steps], axis=1)
+        parts = [(o, slice(i * TOK, (i + 1) * TOK)) for i, o in enumerate(steps)]
         for n, j in enumerate(order_y):
-            c1s[o, n] = nn_dot(wbuf[2 * j + other], hog[block]).astype(jnp.bfloat16)
-            send(c1s.at[o, n], c1r.at[o, n], pair_of(c1_sem, o, n), partner)
+            given = nn_dot(wbuf[2 * j + other], right).astype(jnp.bfloat16)
+            for o, part in parts:
+                c1s[o, n] = given[:, part]
+                send(c1s.at[o, n], c1r.at[o, n], pair_of(c1_sem, o, n), partner)
         for n, j in enumerate(order_y):
-            kept = nn_dot(wbuf[2 * j + core], hog[block])
-            arrived(c1r.at[o, n], pair_of(c1_sem, o, n), partner)
-            c2s[o, n] = (kept + c1r[o, n].astype(jnp.float32)).astype(jnp.bfloat16)
-            sems = (c2_sem.at[0, o, n], c2_sem.at[1, o, y])
-            onward = copy(c2s.at[o, n], c2r.at[o, y], sems, (z, x, j, core))
-            ahead.append((j, onward))
-
-            @pl.when(j != y)
-            def _():
-                onward.start()
-
-            @pl.when(j == y)
-            def _():
-                c2r[o, y] = c2s[o, n]
+            kept = nn_dot(wbuf[2 * j + core], right)
+            for o, part in parts:
+                arrived(c1r.at[o, n], pair_of(c1_sem, o, n), partner)
+                c2s[o, n] = (kept[:, part] + c1r[o, n].astype(jnp.float32)).astype(jnp.bfloat16)
+                sems = (c2_sem.at[0, o, n], c2_sem.at[1, o, y])
+                onward = copy(c2s.at[o, n], c2r.at[o, y], sems, (z, x, j, core))
+                ahead.append((j, onward))
+
+                @pl.when(j != y)
+                def _():
+                    onward.start()
+
+                @pl.when(j == y)
+                def _():
+                    c2r[o, y] = c2s[o, n]
 
     def collect(o):
         for d in (1, 2, 3):
@@ -325,11 +327,14 @@
             c3r[x] = summed.astype(jnp.bfloat16)
 
     project(0)
-    project(1)
+    heads_from(1, 1)
+    heads_from(0, 3)
+    project(1, 3)
     collect(0)
-    project(3)
+    heads_from(0, 2)
+    heads_from(1, 2)
+    project(2)
     collect(1)
-    project(2)
     collect(3)
     collect(2)
     for d in (1, 2, 3):

time: 80.1 us -> 78 us (0.974); the launches traced: 79.1 us -> 77.9 us
  Pallas kernels: 77.5 us -> 76.3 us
    pallas_call x1, Pallas kernels: 77.5 us -> 76.3 us  [local(): pl.pallas_call(kernel, out_shape=jax.ShapeDtypeStruct((TOK, NX * COLS), b...]
where the time goes in v6:
time: 78 us; the launch traced here: 77.9 us
  Pallas kernels  76.3 us (98%)
  local copies, waits for them, and re-layouts  1.65 us (2%)
    pallas_call x1, Pallas kernels, local(): pl.pallas_call(kernel, out_shape=jax.ShapeDtypeStruct((TOK, NX * COLS), b...  76.3 us
    unnamed x1, local copies, waits for them, and re-layouts  1.65 us

profile of v6, /device:TPU:16, one launch (start us, length us, event | category | flops | bytes accessed | tf_op | source)
XLA Modules:
  0.0 77.9 jit_solution(10037725447723679543)
XLA Ops:
  0.0 76.3 %shard_map.82 = bf16[128,896]{1,0:T(8,128)(2,1)} custom-call(bf16[128,512]{1,0:T(8,128)(2,1)} %lat.1, bf16[64,128]{1,0:T(8,128)(2,1)} %bitcast.4, s32[1,64]{1,0:T(1,128)} %bitcast.5, bf16[128,1024]{1,0:T(8,128)(2,1)} %qn_in.1, bf16[128,512]{1,0:T(8,128)(2,1)} %qr_in.1, bf16[512,1024]{1,0:T(8,128)(2,1)} %wuk_in.1, bf16[512,1024]{1,0:T(8,128)(2,1)} %wuv_in.1, ...), custom_call_target="tpu_custom_call" | custom-call | flops 11000000512 | bytes 4000000 | tf_op jit(solution)/shard_map/pallas_call | solution.py:359
  76.3 1.6 %copy.10 = bf16[128,896]{1,0:T(8,128)(2,1)} copy(bf16[128,896]{1,0:T(8,128)(2,1)} %shard_map.82) | data formatting | bytes 458752

commit v7 on v6

--- a/solution.py
+++ b/solution.py
@@ -260,6 +260,9 @@
     serve(3, 0)
     partner_has(1, 2)
 
+    early = list(sent)
+    sent.clear()
+
     for n in range(2):
         half = slice(n * WING, (n + 1) * WING)
         top, total = attend([chunk(1, 2)], n * WING, WING, *state[n])
@@ -281,8 +284,6 @@
     send(passed, passed, pair_of(a_sem, 0, 2), at(dx=-1))
     passed = heads_from(1, 3)
     send(passed, passed, pair_of(a_sem, 1, 2), at(dx=1))
-    for half in range(2):
-        wait_w(7, half)
 
     tilt = 1 - 2 * lax.rem(z, 2)
     order_y = [lax.rem(z // 2 + NY + step, NY) for step in (0, -tilt, tilt, 2)]
@@ -291,27 +292,33 @@
     def project(*steps):
         right = jnp.concatenate([hog[lax.rem(x + o, NX)] for o in steps], axis=1)
         parts = [(o, slice(i * TOK, (i + 1) * TOK)) for i, o in enumerate(steps)]
-        for n, j in enumerate(order_y):
-            given = nn_dot(wbuf[2 * j + other], right).astype(jnp.bfloat16)
-            for o, part in parts:
-                c1s[o, n] = given[:, part]
-                send(c1s.at[o, n], c1r.at[o, n], pair_of(c1_sem, o, n), partner)
-        for n, j in enumerate(order_y):
-            kept = nn_dot(wbuf[2 * j + core], right)
-            for o, part in parts:
-                arrived(c1r.at[o, n], pair_of(c1_sem, o, n), partner)
-                c2s[o, n] = (kept[:, part] + c1r[o, n].astype(jnp.float32)).astype(jnp.bfloat16)
-                sems = (c2_sem.at[0, o, n], c2_sem.at[1, o, y])
-                onward = copy(c2s.at[o, n], c2r.at[o, y], sems, (z, x, j, core))
-                ahead.append((j, onward))
-
-                @pl.when(j != y)
-                def _():
-                    onward.start()
-
-                @pl.when(j == y)
-                def _():
-                    c2r[o, y] = c2s[o, n]
+        for some in ((0, 1, 2), (3,)) if 0 in steps else (range(NY),):
+            if some == (3,):
+                for made in early:
+                    made.wait_send()
+                for half in range(2):
+                    wait_w(7, half)
+            for n, j in [(n, order_y[n]) for n in some]:
+                given = nn_dot(wbuf[2 * j + other], right).astype(jnp.bfloat16)
+                for o, part in parts:
+                    c1s[o, n] = given[:, part]
+                    send(c1s.at[o, n], c1r.at[o, n], pair_of(c1_sem, o, n), partner)
+            for n, j in [(n, order_y[n]) for n in some]:
+                kept = nn_dot(wbuf[2 * j + core], right)
+                for o, part in parts:
+                    arrived(c1r.at[o, n], pair_of(c1_sem, o, n), partner)
+                    c2s[o, n] = (kept[:, part] + c1r[o, n].astype(jnp.float32)).astype(jnp.bfloat16)
+                    sems = (c2_sem.at[0, o, n], c2_sem.at[1, o, y])
+                    onward = copy(c2s.at[o, n], c2r.at[o, y], sems, (z, x, j, core))
+                    ahead.append((j, onward))
+
+                    @pl.when(j != y)
+                    def _():
+                        onward.start()
+
+                    @pl.when(j == y)
+                    def _():
+                        c2r[o, y] = c2s[o, n]
 
     def collect(o):
         for d in (1, 2, 3):

time: 78 us -> 78.7 us (level)
  no operation moved by 1% of the time
where the time goes in v7:
time: 78.7 us; the launch traced here: 78.5 us
  Pallas kernels  76.9 us (98%)
  local copies, waits for them, and re-layouts  1.65 us (2%)
    pallas_call x1, Pallas kernels, local(): pl.pallas_call(kernel, out_shape=jax.ShapeDtypeStruct((TOK, NX * COLS), b...  76.9 us
    unnamed x1, local copies, waits for them, and re-layouts  1.65 us

profile of v7, /device:TPU:16, one launch (start us, length us, event | category | flops | bytes accessed | tf_op | source)
XLA Modules:
  0.0 78.5 jit_solution(14347804092354150836)
XLA Ops:
  0.0 76.9 %shard_map.82 = bf16[128,896]{1,0:T(8,128)(2,1)} custom-call(bf16[128,512]{1,0:T(8,128)(2,1)} %lat.1, bf16[64,128]{1,0:T(8,128)(2,1)} %bitcast.4, s32[1,64]{1,0:T(1,128)} %bitcast.5, bf16[128,1024]{1,0:T(8,128)(2,1)} %qn_in.1, bf16[128,512]{1,0:T(8,128)(2,1)} %qr_in.1, bf16[512,1024]{1,0:T(8,128)(2,1)} %wuk_in.1, bf16[512,1024]{1,0:T(8,128)(2,1)} %wuv_in.1, ...), custom_call_target="tpu_custom_call" | custom-call | flops 11000000512 | bytes 4000000 | tf_op jit(solution)/shard_map/pallas_call | solution.py:366
  76.9 1.6 %copy.10 = bf16[128,896]{1,0:T(8,128)(2,1)} copy(bf16[128,896]{1,0:T(8,128)(2,1)} %shard_map.82) | data formatting | bytes 458752
